TPU v7x, 32 devices: a whole 2x2x4 slice. The times are simulated.
32 devices in a mesh: seq: 8 (over y, x, core), head: 4 (over z).
Axes of the slice: x: 2, y: 2, z: 4, core: 2. Of those that a mesh axis runs over, the one named last changes fastest.
Arguments:
- inputs: bfloat16 [4096, 4096], P('seq'), may hold values from -6 to 6
- q_weight: bfloat16 [4096, 2048], P(None, 'head'), may hold values from -0.09375 to 0.09375
- kv_weight: bfloat16 [4096, 2, 512], P(None, None, 'head'), may hold values from -0.09375 to 0.09375
- norm_gain: float32 [2048], P('head'), may hold values from 0.1 to 1.9
- out_grad: bfloat16 [4096, 2048], P('seq', 'head'), may hold values from -6 to 6
Outputs:
- input_grad: bfloat16 [4096, 4096], P('seq', 'head')
- q_weight_grad: float32 [4096, 2048], P('seq', 'head')
- kv_weight_grad: float32 [4096, 2, 512], P('seq', None, 'head')
All inputs are finite; a program needn't handle non-finite values.
Results may differ from a plain program's by a relative error of at most 0.022.
Values may be sent and summed in bfloat16 or wider, within the bound.
No kernel may reach another device: no remote copies, remote signals or barrier semaphores. Data moves between devices by JAX's collectives and lax.ppermute only.
A program may use at most 128 MiB of HBM per device.

v0:
```python
import jax
import jax.numpy as jnp
from jax import lax
from jax.sharding import PartitionSpec as P

HD = 128


exact_prec = lax.Precision.HIGHEST
EPSILON = 1e-05


def entering(shard, axis, join, neutral):
    place = lax.axis_index(axis)
    gathered = lax.all_gather(shard.astype(jnp.bfloat16), axis)
    state = jnp.zeros_like(shard) + jnp.asarray(neutral, shard.dtype)

    def one(lap, state):
        return join(state, lax.dynamic_index_in_dim(gathered, lap, 0, False).astype(shard.dtype))

    return lax.fori_loop(0, place, one, state)


def entering_2(shard, axis, join, neutral):
    count = lax.axis_size(axis)
    place = lax.axis_index(axis)
    ahead = count - 1 - place
    gathered = lax.all_gather(
        shard.astype(jnp.bfloat16 if shard.dtype == jnp.float32 else shard.dtype), axis
    )
    state = jnp.zeros_like(shard) + jnp.asarray(neutral, shard.dtype)

    def one(lap, state):
        source = count - 1 - lap
        return join(state, lax.dynamic_index_in_dim(gathered, source, 0, False).astype(shard.dtype))

    return lax.fori_loop(0, ahead, one, state)


def causal_mask(length):
    row_ids = lax.broadcasted_iota(jnp.int32, (length, length), 0)
    column_ids = lax.broadcasted_iota(jnp.int32, (length, length), 1)
    return (column_ids <= row_ids).astype(jnp.float32)


def add_states(earlier, later):
    return earlier + later


def body(inputs, q_weight, kv_weight, norm_gain, out_grad):
    tok_count = inputs.shape[0]
    q_cols = q_weight.shape[1]
    kv_cols = kv_weight.shape[2]
    kv_here = kv_cols // HD
    per_group = q_cols // HD // kv_here
    joined_weight = jnp.concatenate([q_weight, kv_weight[:, 0, :], kv_weight[:, 1, :]], axis=1)
    projected = jnp.dot(inputs, joined_weight, preferred_element_type=jnp.float32).astype(
        jnp.bfloat16
    )
    queries = projected[:, :q_cols].astype(jnp.float32).reshape(tok_count, kv_here, per_group, HD)
    key_rows = (
        projected[:, q_cols : q_cols + kv_cols].astype(jnp.float32).reshape(tok_count, kv_here, HD)
    )
    val_rows = projected[:, q_cols + kv_cols :].astype(jnp.float32).reshape(tok_count, kv_here, HD)
    tri_mask = causal_mask(tok_count)
    own_state = jnp.einsum("sgi,sgj->gij", key_rows, val_rows, precision=exact_prec)
    zero_state = jnp.zeros_like(own_state)
    earlier = entering(own_state, "seq", add_states, zero_state)
    scores = jnp.einsum("tghi,sgi->ghts", queries, key_rows, precision=exact_prec) * tri_mask
    attended = jnp.einsum("ghts,sgj->tghj", scores, val_rows, precision=exact_prec)
    attended = attended + jnp.einsum("tghi,gij->tghj", queries, earlier, precision=exact_prec)
    inv_rms = lax.rsqrt(jnp.mean(attended * attended, axis=-1, keepdims=True) + EPSILON)
    gain_heads = norm_gain.reshape(kv_here, per_group, HD)
    scaled_grad = gain_heads * out_grad.astype(jnp.float32).reshape(
        tok_count, kv_here, per_group, HD
    )
    along = jnp.mean(scaled_grad * attended, axis=-1, keepdims=True)
    attn_grad = inv_rms * (scaled_grad - attended * (inv_rms * inv_rms) * along)
    grad_scores = jnp.einsum("tghj,sgj->ghts", attn_grad, val_rows, precision=exact_prec) * tri_mask
    query_grad = jnp.einsum("ghts,sgi->tghi", grad_scores, key_rows, precision=exact_prec)
    query_grad = query_grad + jnp.einsum("tghj,gij->tghi", attn_grad, earlier, precision=exact_prec)
    own_grad = jnp.einsum("tghi,tghj->gij", queries, attn_grad, precision=exact_prec)
    later = entering_2(own_grad, "seq", add_states, zero_state)
    key_grad = jnp.einsum("ghts,tghi->sgi", grad_scores, queries, precision=exact_prec)
    key_grad = key_grad + jnp.einsum("sgj,gij->sgi", val_rows, later, precision=exact_prec)
    val_grad = jnp.einsum("ghts,tghj->sgj", scores, attn_grad, precision=exact_prec)
    val_grad = val_grad + jnp.einsum("sgi,gij->sgj", key_rows, later, precision=exact_prec)
    all_grads = jnp.concatenate(
        [
            query_grad.reshape(tok_count, q_cols),
            key_grad.reshape(tok_count, kv_cols),
            val_grad.reshape(tok_count, kv_cols),
        ],
        axis=1,
    ).astype(jnp.bfloat16)
    partial_input = jnp.dot(all_grads, joined_weight.T, preferred_element_type=jnp.float32)
    input_grad = lax.psum_scatter(
        partial_input.astype(jnp.bfloat16), "head", scatter_dimension=1, tiled=True
    )
    joined = lax.psum_scatter(
        jnp.dot(inputs.T, all_grads, preferred_element_type=jnp.float32).astype(jnp.bfloat16),
        "seq",
        scatter_dimension=0,
        tiled=True,
    ).astype(jnp.float32)
    q_weight_grad = joined[:, :q_cols]
    kv_weight_grad = joined[:, q_cols:].reshape(joined.shape[0], 2, kv_cols)
    return (input_grad, q_weight_grad, kv_weight_grad)


def solution(mesh):
    return jax.shard_map(
        body,
        mesh=mesh,
        in_specs=(
            P("seq", None),
            P(None, "head"),
            P(None, None, "head"),
            P("head"),
            P("seq", "head"),
        ),
        out_specs=(P("seq", "head"), P("seq", "head"), P("seq", None, "head")),
        check_vma=False,
    )
```

profile of v0, /device:TPU:0, one launch (start us, length us, event | category | flops | bytes accessed | tf_op | source)
XLA Modules:
  0.0 230.3 jit_solution(10122910358469268766)
XLA Ops:
  7.2 0.1 fusion.43
  7.3 5.7 %fusion.65 = (bf16[4096,1,128]{2,1,0:T(2,128)(2,1)S(1)}, bf16[4096,1,128]{2,1,0:T(2,128)(2,1)S(1)}) fusion(bf16[4096,2,128]{2,1,0:T(2,128)(2,1)} %param.11), kind=kLoop, calls=%fused_computation.75 | loop fusion | bytes 4194304 | tf_op jit(solution)/shard_map/slice | solution.py:56
  13.1 0.3 copy_bitcast_fusion
  13.4 0.9 copy-done.5
  14.3 1.7 copy-done.14
  16.0 3.5 %fusion.25 = bf16[512,768]{0,1:T(8,128)(2,1)S(1)} fusion(bf16[512,4096]{1,0:T(8,128)(2,1)S(1)} %copy-done.14, bf16[4096,128]{1,0:T(8,128)(2,1)S(1)} %get-tuple-element.129, bf16[4096,128]{1,0:T(8,128)(2,1)S(1)} %get-tuple-element.130, bf16[4096,512]{1,0:T(8,128)(2,1)S(1)} %copy-done.15), kind=kOutput, calls=%fused_computation.26 | convolution fusion | flops 3240493056 | bytes 11272192 | tf_op jit(solution)/shard_map/dot_general | solution.py:57
  19.5 0.2 convolution_convert_fusion.2
  19.7 2.7 %fusion.46 = f32[512,512,4]{1,0,2:T(8,128)} fusion(bf16[512,4,128]{0,2,1:T(8,128)(2,1)S(1)} %bitcast.154, bf16[512,768]{0,1:T(8,128)(2,1)S(1)} %fusion.25), kind=kOutput, calls=%fused_computation.54 | convolution fusion | flops 268435456 | bytes 4849664 | tf_op jit(solution)/shard_map/tghi,sgi->ghts/dot_general | solution.py:69
  22.4 1.3 copy.33
  23.7 11.9 %all-gather = bf16[1024,128]{1,0:T(8,128)(2,1)} all-gather(bf16[128,128]{1,0:T(8,128)(2,1)S(1)} %convolution_convert_fusion.2), channel_id=2, replica_groups=mesh['seq'=8,'head'=4] {'seq'}, dimensions={0}, use_global_device_ids=true | all-gather | bytes 294912 | tf_op jit(solution)/shard_map/all_gather | solution.py:15
  35.6 4.0 %fusion.20 = f32[512,1,4,128]{0,3,2,1:T(8,128)S(1)} fusion(f32[512,512,4]{1,0,2:T(8,128)} %fusion.46, f32[512,512]{0,1:T(8,128)S(1)} %fusion.43, bf16[512,768]{0,1:T(8,128)(2,1)S(1)} %fusion.25), kind=kOutput, calls=%fused_computation.23 | convolution fusion | flops 1611661312 | bytes 6422528 | tf_op jit(solution)/shard_map/ghts,sgj->tghj/dot_general | solution.py:70
  39.6 0.9 multiply_reduce_fusion.1
  40.6 1.8 subtract_multiply_fusion
  42.3 5.1 %fusion.30 = f32[128,512]{1,0:T(8,128)} fusion(f32[512,512,4]{1,0,2:T(8,128)S(1)} %copy-done, f32[512,512]{0,1:T(8,128)S(1)} %fusion.43, f32[512,1,4,128]{0,3,2,1:T(8,128)S(1)} %subtract_multiply_fusion), kind=kOutput, calls=%fused_computation.31 | convolution fusion | flops 1611661312 | bytes 6553600 | tf_op jit(solution)/shard_map/ghts,tghj->sgj/dot_general | solution.py:86
  47.5 0.7 fusion.37
  48.1 1.9 fusion.41
  50.0 3.3 %fusion.27 = f32[128,512]{1,0:T(8,128)} fusion(bf16[512,4,128]{0,2,1:T(8,128)(2,1)S(1)} %bitcast.157, f32[512,512,4]{1,0,2:T(8,128)S(1)} %fusion.41, f32[512,512]{0,1:T(8,128)S(1)} %fusion.43), kind=kOutput, calls=%fused_computation.30 | convolution fusion | flops 1611661312 | bytes 6029312 | tf_op jit(solution)/shard_map/ghts,tghi->sgi/dot_general | solution.py:84
  53.3 3.1 %fusion.17 = f32[512,1,4,128]{0,3,2,1:T(8,128)} fusion(f32[512,512,4]{1,0,2:T(8,128)S(1)} %fusion.41, f32[512,512]{0,1:T(8,128)S(1)} %fusion.43, bf16[512,768]{0,1:T(8,128)(2,1)S(1)} %fusion.25), kind=kOutput, calls=%fused_computation.22 | convolution fusion | flops 1611661312 | bytes 6422528 | tf_op jit(solution)/shard_map/ghts,sgi->tghi/dot_general | solution.py:80
  56.4 13.9 %all-gather.1 = bf16[1024,128]{1,0:T(8,128)(2,1)S(1)} all-gather(bf16[128,128]{1,0:T(8,128)(2,1)S(1)} %fusion.37), channel_id=3, replica_groups=mesh['seq'=8,'head'=4] {'seq'}, dimensions={0}, use_global_device_ids=true | all-gather | bytes 294912 | tf_op jit(solution)/shard_map/all_gather | solution.py:28
  70.3 0.3 while.23
  70.5 0.3 fusion.35
  70.9 0.3 fusion.36
  71.2 2.3 fusion.26
  73.5 8.3 %fusion = bf16[4096,768]{0,1:T(8,128)(2,1)} fusion(bf16[512,4096]{1,0:T(8,128)(2,1)} %param.9, bf16[512,128]{0,1:T(8,128)(2,1)S(1)} %fusion.35, bf16[512,128]{0,1:T(8,128)(2,1)S(1)} %fusion.36, bf16[512,512]{0,1:T(8,128)(2,1)S(1)} %bitcast.162), kind=kOutput, calls=%fused_computation.4 | convolution fusion | flops 3226730496 | bytes 11272192 | tf_op jit(solution)/shard_map/dot_general | solution.py:101
  81.8 1.1 copy-done.6
  83.0 0.3 copy-done.8
  83.3 7.8 %convolution_convert_fusion.1 = bf16[512,4096]{1,0:T(8,128)(2,1)} fusion(bf16[4096,128]{1,0:T(8,128)(2,1)S(1)} %copy-done.6, bf16[4096,128]{1,0:T(8,128)(2,1)S(1)} %copy-done.8, bf16[4096,512]{1,0:T(8,128)(2,1)} %param.10, bf16[512,128]{0,1:T(8,128)(2,1)S(1)} %copy-done.10, bf16[512,128]{0,1:T(8,128)(2,1)S(1)} %copy-done.12, bf16[512,512]{0,1:T(8,128)(2,1)S(1)} %bitcast.163), kind=kOutput, calls=%fused_computation.5 | convolution fusion | flops 3244556288 | bytes 11272192 | tf_op jit(solution)/shard_map/dot_general | solution.py:96
  91.1 52.6 %reduce-scatter.5.cloned.1.call-done = bf16[512,768]{0,1:T(8,128)(2,1)} async-done(((bf16[4096,768]{0,1:T(8,128)(2,1)}), bf16[512,768]{0,1:T(8,128)(2,1)}) %reduce-scatter.5.cloned.1.call-update) | async-done | bytes 786448 | tf_op jit(solution)/shard_map/reduce_scatter | solution.py:100
  143.7 1.2 slice.31
  145.0 1.3 copy.42
  146.3 1.0 copy.43
  147.3 76.1 %reduce-scatter.3.cloned.1.call-done = bf16[512,1024]{1,0:T(8,128)(2,1)} async-done(((bf16[512,4096]{1,0:T(8,128)(2,1)}), bf16[512,1024]{1,0:T(8,128)(2,1)}) %reduce-scatter.3.cloned.1.call-update) | async-done | bytes 1048592 | tf_op jit(solution)/shard_map/reduce_scatter | solution.py:97
  (46 shorter events, 0.4 us)
Async XLA Ops:
  7.2 136.6 %reduce-scatter.5.cloned.1.call-start = ((), (), s32[]{:S(2)}) async-start(), calls=%async_computation.3 | async-start | bytes 7077888 | tf_op jit(solution)/shard_map/reduce_scatter | solution.py:100
  7.3 7.0 %copy-start.15 = (bf16[4096,512]{1,0:T(8,128)(2,1)S(1)}, bf16[4096,512]{1,0:T(8,128)(2,1)}, u32[]{:S(2)}) copy-start(bf16[4096,512]{1,0:T(8,128)(2,1)} %param.10) | copy-start | bytes 12582916
  13.0 2.9 %copy-start.14 = (bf16[512,4096]{1,0:T(8,128)(2,1)S(1)}, bf16[512,4096]{1,0:T(8,128)(2,1)}, u32[]{:S(2)}) copy-start(bf16[512,4096]{1,0:T(8,128)(2,1)} %param.9) | copy-start | bytes 12582916
  13.3 1.0 copy-start.5
  13.3 6.1 %copy-start.7 = (bf16[4096,128]{1,0:T(8,128)(2,1)}, bf16[4096,128]{1,0:T(8,128)(2,1)S(1)}, u32[]{:S(2)}) copy-start(bf16[4096,128]{1,0:T(8,128)(2,1)S(1)} %get-tuple-element.130) | copy-start | bytes 3145732
  23.7 16.9 %copy-start.1 = (f32[512,512]{0,1:T(8,128)}, f32[512,512]{0,1:T(8,128)S(1)}, u32[]{:S(2)}) copy-start(f32[512,512]{0,1:T(8,128)S(1)} %copy.33) | copy-start | bytes 3145732
  23.7 16.0 %copy-start.13 = (f32[512]{0:T(512)S(1)}, f32[512]{0:T(512)}, u32[]{:S(2)}) copy-start(f32[512]{0:T(512)} %param.12) | copy-start | bytes 6148
  39.6 2.7 %copy-start = (f32[512,512,4]{1,0,2:T(8,128)S(1)}, f32[512,512,4]{1,0,2:T(8,128)}, u32[]{:S(2)}) copy-start(f32[512,512,4]{1,0,2:T(8,128)} %fusion.46) | copy-start | bytes 12582916
  53.3 17.2 %copy-start.3 = (f32[128,512]{1,0:T(8,128)S(1)}, f32[128,512]{1,0:T(8,128)}, u32[]{:S(2)}) copy-start(f32[128,512]{1,0:T(8,128)} %fusion.30) | copy-start | bytes 786436
  53.3 17.6 %copy-start.4 = (f32[128,512]{1,0:T(8,128)S(1)}, f32[128,512]{1,0:T(8,128)}, u32[]{:S(2)}) copy-start(f32[128,512]{1,0:T(8,128)} %fusion.27) | copy-start | bytes 786436
  70.9 2.6 %copy-start.9 = (bf16[512,128]{0,1:T(8,128)(2,1)}, bf16[512,128]{0,1:T(8,128)(2,1)S(1)}, u32[]{:S(2)}) copy-start(bf16[512,128]{0,1:T(8,128)(2,1)S(1)} %fusion.35) | copy-start | bytes 393220
  71.2 2.3 %copy-start.11 = (bf16[512,128]{0,1:T(8,128)(2,1)}, bf16[512,128]{0,1:T(8,128)(2,1)S(1)}, u32[]{:S(2)}) copy-start(bf16[512,128]{0,1:T(8,128)(2,1)S(1)} %fusion.36) | copy-start | bytes 393220
  81.7 1.2 copy-start.6
  81.7 1.5 copy-start.8
  81.7 1.5 copy-start.10
  81.7 1.6 copy-start.12
  81.8 141.7 %reduce-scatter.3.cloned.1.call-start = ((), (), s32[]{:S(2)}) async-start(), calls=%async_computation.2 | async-start | bytes 5242880 | tf_op jit(solution)/shard_map/reduce_scatter | solution.py:97
  143.7 2.6 %copy-start.2 = (bf16[512,768]{0,1:T(8,128)(2,1)S(1)}, bf16[512,768]{0,1:T(8,128)(2,1)}, u32[]{:S(2)}) copy-start(bf16[512,768]{0,1:T(8,128)(2,1)} %reduce-scatter.5.cloned.1.call-done) | copy-start | bytes 2359300
Sparse Core Ops, SparseCore 0:
  81.9 61.7 reduce-scatter.4
  146.7 76.7 reduce-scatter.2
where the time goes:
time: 231 us; the launch traced here: 230 us
  waiting for transfers between devices  129 us (56%)
  matrix products  44.1 us (19%)
  blocking collectives  25.8 us (11%)
  local copies, waits for them, and re-layouts  15 us (6%)
  between operations  14.3 us (6%)
    reduce_scatter x1, waiting for transfers between devices, body(): lax.psum_scatter(partial_input.astype(jnp.bfloat16), 'head', scatter_dime...  76.1 us
    reduce_scatter x1, waiting for transfers between devices, body(): lax.psum_scatter(jnp.dot(inputs.T, all_grads, preferred_element_type=jnp....  52.6 us
    all_gather x1, blocking collectives, entering_2(): lax.all_gather(shard.astype(jnp.bfloat16 if shard.dtype == jnp.float32 el...  13.9 us
    all_gather x1, blocking collectives, entering(): gathered = lax.all_gather(shard.astype(jnp.bfloat16), axis)  11.9 us
    dot_general x1, matrix products, body(): jnp.dot(inputs.T, all_grads, preferred_element_type=jnp.float32)  8.26 us
    dot_general x1, matrix products, body(): jnp.dot(all_grads, joined_weight.T, preferred_element_type=jnp.float32)  7.77 us
    unnamed x34, local copies, waits for them, and re-layouts  6.49 us
    slice x1, local copies, waits for them, and re-layouts, body(): kv_weight[:, 0, :]  5.69 us
  transfers between devices with their start and end apart: 2, of which 2 were waited for; matrix products, arithmetic and copies ran while one was open for 5% of the time, Pallas kernels for 0%

commit v1 on v0

v1 whole, which is shorter than its diff:
```python
import functools

import jax
import jax.numpy as jnp
from jax import lax
from jax.experimental import pallas as pl
from jax.experimental.pallas import tpu as pltpu
from jax.sharding import PartitionSpec as P

HD = 128
EPSILON = 1e-05
F32 = jnp.float32
BF16 = jnp.bfloat16
VMEM_LIMIT = 40 * 1024 * 1024


def mm(a, b):
    return jnp.dot(a, b, preferred_element_type=F32)


def mm_nt(a, b):
    return lax.dot_general(a, b, (((1,), (1,)), ((), ())), preferred_element_type=F32)


def mm_tn(a, b):
    return lax.dot_general(a, b, (((0,), (0,)), ((), ())), preferred_element_type=F32)


def params():
    return pltpu.CompilerParams(vmem_limit_bytes=VMEM_LIMIT)


def cost(flops, nbytes):
    return pl.CostEstimate(flops=int(flops), bytes_accessed=int(nbytes), transcendentals=0)


VSPEC = pl.BlockSpec(memory_space=pltpu.VMEM)
SSPEC = pl.BlockSpec(memory_space=pltpu.SMEM)


def kv_kernel(x_ref, w_ref, kv_ref, state_ref, wkv_ref, acc_ref):
    step = pl.program_id(0)
    steps = pl.num_programs(0)
    rows = 2 * HD
    row = lax.broadcasted_iota(jnp.int32, (rows, rows), 0)
    col = lax.broadcasted_iota(jnp.int32, (rows, rows), 1)
    target = jnp.where(row < HD, 2 * row, 2 * (row - HD) + 1)
    perm = jnp.where(col == target, 1.0, 0.0).astype(BF16)
    for i in range(w_ref.shape[0] // rows):
        both = mm(perm, w_ref[i * rows : (i + 1) * rows, :]).astype(BF16)
        wkv_ref[i * HD : (i + 1) * HD, :HD] = both[:HD]
        wkv_ref[i * HD : (i + 1) * HD, HD:] = both[HD:]
    part = mm(x_ref[...], wkv_ref[...])

    @pl.when(step == 0)
    def _():
        acc_ref[...] = part

    @pl.when(step > 0)
    def _():
        acc_ref[...] += part

    @pl.when(step == steps - 1)
    def _():
        kv = acc_ref[...].astype(BF16)
        kv_ref[...] = kv
        state_ref[...] = mm_tn(kv[:, :HD], kv[:, HD:]).astype(BF16)


def kv_project(x, kv_flat):
    tok, d = x.shape
    steps = 4
    blk = d // steps
    return pl.pallas_call(
        kv_kernel,
        grid=(steps,),
        in_specs=[
            pl.BlockSpec((tok, blk), lambda i: (0, i)),
            pl.BlockSpec((2 * blk, HD), lambda i: (i, 0)),
        ],
        out_specs=[
            pl.BlockSpec((tok, 2 * HD), lambda i: (0, 0)),
            pl.BlockSpec((HD, HD), lambda i: (0, 0)),
            pl.BlockSpec((blk, 2 * HD), lambda i: (i, 0)),
        ],
        out_shape=[
            jax.ShapeDtypeStruct((tok, 2 * HD), BF16),
            jax.ShapeDtypeStruct((HD, HD), BF16),
            jax.ShapeDtypeStruct((d, 2 * HD), BF16),
        ],
        scratch_shapes=[pltpu.VMEM((tok, 2 * HD), F32)],
        compiler_params=params(),
        cost_estimate=cost(4 * tok * d * HD, 2 * (tok * d + 4 * d * HD)),
        name="kv_project",
    )(x, kv_flat)


def halves(tok):
    blk = min(256, tok)
    return [(lo, lo + blk) for lo in range(0, tok, blk)]


def masked(scores, row_first):
    rows, cols = scores.shape
    row = lax.broadcasted_iota(jnp.int32, (rows, cols), 0) + row_first
    col = lax.broadcasted_iota(jnp.int32, (rows, cols), 1)
    return jnp.where(col <= row, scores, 0.0)


def q_kernel(x_ref, w_ref, kv_ref, q_ref, o_ref, acc_ref):
    step = pl.program_id(0)
    steps = pl.num_programs(0)
    part = mm(x_ref[...], w_ref[...])

    @pl.when(step == 0)
    def _():
        acc_ref[...] = part

    @pl.when((step > 0) & (step < steps - 1))
    def _():
        acc_ref[...] += part

    @pl.when(step == steps - 1)
    def _():
        q = (acc_ref[...] + part).astype(BF16)
        q_ref[...] = q
        k, v = kv_ref[:, :HD], kv_ref[:, HD:]
        for lo, hi in halves(q.shape[0]):
            for h in range(q.shape[1] // HD):
                s = masked(mm_nt(q[lo:hi, h * HD : (h + 1) * HD], k[:hi]), lo)
                o_ref[lo:hi, h * HD : (h + 1) * HD] = mm(s.astype(BF16), v[:hi])


def q_project(x, q_weight, kv):
    tok, d = x.shape
    cols = q_weight.shape[1]
    steps = 4
    blk = d // steps
    return pl.pallas_call(
        q_kernel,
        grid=(steps,),
        in_specs=[
            pl.BlockSpec((tok, blk), lambda i: (0, i)),
            pl.BlockSpec((blk, cols), lambda i: (i, 0)),
            pl.BlockSpec((tok, 2 * HD), lambda i: (0, 0)),
        ],
        out_specs=[
            pl.BlockSpec((tok, cols), lambda i: (0, 0)),
            pl.BlockSpec((tok, cols), lambda i: (0, 0)),
        ],
        out_shape=[
            jax.ShapeDtypeStruct((tok, cols), BF16),
            jax.ShapeDtypeStruct((tok, cols), F32),
        ],
        scratch_shapes=[pltpu.VMEM((tok, cols), F32)],
        compiler_params=params(),
        cost_estimate=cost(2 * tok * d * cols, 2 * (tok * d + d * cols)),
        name="q_project",
    )(x, q_weight, kv)


def weighted(bits_ref, refs):
    total = None
    for i, ref in enumerate(refs):
        term = ref[...].astype(F32) * bits_ref[i].astype(F32)
        total = term if total is None else total + term
    return total


def grad_kernel(n, bits_ref, q_ref, o_ref, kv_ref, gain_ref, up_ref, *refs):
    states, (dq_ref, do_ref, own_ref) = refs[:n], refs[n:]
    prev = weighted(bits_ref, states).astype(BF16)
    k, v = kv_ref[:, :HD], kv_ref[:, HD:]
    own = None
    for lo, hi in halves(q_ref.shape[0]):
        for h in range(q_ref.shape[1] // HD):
            c = slice(h * HD, (h + 1) * HD)
            q = q_ref[lo:hi, c]
            o = o_ref[lo:hi, c] + mm(q, prev)
            inv = lax.rsqrt(jnp.mean(o * o, axis=-1, keepdims=True) + EPSILON)
            scaled = gain_ref[:, c] * up_ref[lo:hi, c].astype(F32)
            along = jnp.mean(scaled * o, axis=-1, keepdims=True)
            do = (inv * (scaled - o * ((inv * inv) * along))).astype(BF16)
            do_ref[lo:hi, c] = do
            s = masked(mm_nt(do, v[:hi]), lo).astype(BF16)
            dq_ref[lo:hi, c] = (mm(s, k[:hi]) + mm_nt(do, prev)).astype(BF16)
            part = mm_tn(q, do)
            own = part if own is None else own + part
    own_ref[...] = own.astype(BF16)


def grad_step(bits, q, o, kv, gain, upstream, states):
    tok, cols = q.shape
    n = len(states)
    return pl.pallas_call(
        functools.partial(grad_kernel, n),
        in_specs=[SSPEC] + [VSPEC] * (5 + n),
        out_specs=[VSPEC] * 3,
        out_shape=[
            jax.ShapeDtypeStruct((tok, cols), BF16),
            jax.ShapeDtypeStruct((tok, cols), BF16),
            jax.ShapeDtypeStruct((HD, HD), BF16),
        ],
        compiler_params=params(),
        cost_estimate=cost(8 * tok * tok * cols, 12 * tok * cols),
        name="grad_step",
    )(bits, q, o, kv, gain.reshape(1, cols), upstream, *states)


def inner_kernel(q_ref, do_ref, kv_ref, out_ref):
    k, v = kv_ref[:, :HD], kv_ref[:, HD:]
    tok = q_ref.shape[0]
    for lo, hi in halves(tok):
        col = lax.broadcasted_iota(jnp.int32, (hi - lo, tok - lo), 1)
        row = lax.broadcasted_iota(jnp.int32, (hi - lo, tok - lo), 0)
        dk = dv = None
        for h in range(q_ref.shape[1] // HD):
            c = slice(h * HD, (h + 1) * HD)
            q, do = q_ref[lo:, c], do_ref[lo:, c]
            s = jnp.where(col >= row, mm_nt(k[lo:hi], q), 0.0).astype(BF16)
            ds = jnp.where(col >= row, mm_nt(v[lo:hi], do), 0.0).astype(BF16)
            dk_h, dv_h = mm(ds, q), mm(s, do)
            dk = dk_h if dk is None else dk + dk_h
            dv = dv_h if dv is None else dv + dv_h
        out_ref[lo:hi, :HD] = dk
        out_ref[lo:hi, HD:] = dv


def inner_step(q, do, kv):
    tok, cols = q.shape
    return pl.pallas_call(
        inner_kernel,
        in_specs=[VSPEC] * 3,
        out_specs=VSPEC,
        out_shape=jax.ShapeDtypeStruct((tok, 2 * HD), F32),
        compiler_params=params(),
        cost_estimate=cost(8 * tok * tok * cols, 8 * tok * cols),
        name="inner_step",
    )(q, do, kv)


def outer_kernel(n, bits_ref, inner_ref, kv_ref, *refs):
    states, out_ref = refs[:n], refs[n]
    later = weighted(bits_ref, states).astype(BF16)
    k, v = kv_ref[:, :HD], kv_ref[:, HD:]
    out_ref[:, :HD] = (inner_ref[:, :HD] + mm_nt(v, later)).astype(BF16)
    out_ref[:, HD:] = (inner_ref[:, HD:] + mm(k, later)).astype(BF16)


def outer_step(bits, inner, kv, states):
    tok = kv.shape[0]
    n = len(states)
    return pl.pallas_call(
        functools.partial(outer_kernel, n),
        in_specs=[SSPEC] + [VSPEC] * (2 + n),
        out_specs=VSPEC,
        out_shape=jax.ShapeDtypeStruct((tok, 2 * HD), BF16),
        compiler_params=params(),
        cost_estimate=cost(4 * tok * HD * HD, 8 * tok * HD),
        name="outer_step",
    )(bits, inner, kv, *states)


def send_kernel(ids_ref, x_ref, g_ref, out_ref, gt_ref):
    @pl.when(pl.program_id(0) == 0)
    def _():
        gt_ref[...] = g_ref[...].T

    out_ref[0] = mm(gt_ref[...], x_ref[...]).astype(BF16)


def weight_send(ids, x, g, count):
    tok, d = x.shape
    cols = g.shape[1]
    blk = d // (2 * count)
    return pl.pallas_call(
        send_kernel,
        grid_spec=pltpu.PrefetchScalarGridSpec(
            num_scalar_prefetch=1,
            grid=(count,),
            in_specs=[
                pl.BlockSpec((tok, blk), lambda i, ids: (0, ids[i])),
                pl.BlockSpec((tok, cols), lambda i, ids: (0, 0)),
            ],
            out_specs=pl.BlockSpec((1, cols, blk), lambda i, ids: (i, 0, 0)),
            scratch_shapes=[pltpu.VMEM((cols, tok), BF16)],
        ),
        out_shape=jax.ShapeDtypeStruct((count, cols, blk), BF16),
        compiler_params=params(),
        cost_estimate=cost(2 * tok * cols * blk * count, 2 * count * blk * (tok + cols)),
        name="weight_send",
    )(ids, x, g)


def keep_kernel(half, ids_ref, x_ref, g_ref, got_ref, high_ref, low_ref, gt_ref):
    step = pl.program_id(0)

    @pl.when(step == 0)
    def _():
        gt_ref[...] = g_ref[...].T

    total = mm(gt_ref[...], x_ref[...]) + got_ref[0].astype(F32)

    @pl.when(step < half)
    def _():
        high_ref[0] = total.astype(BF16)

    @pl.when(step >= half)
    def _():
        low_ref[0] = total.astype(BF16)


def weight_keep(ids, x, g, got, count):
    tok, d = x.shape
    cols = g.shape[1]
    blk = d // (2 * count)
    half = count // 2
    where = lambda i: jnp.where(i < half, i + half, i - half)
    return pl.pallas_call(
        functools.partial(keep_kernel, half),
        grid_spec=pltpu.PrefetchScalarGridSpec(
            num_scalar_prefetch=1,
            grid=(count,),
            in_specs=[
                pl.BlockSpec((tok, blk), lambda i, ids: (0, ids[where(i)])),
                pl.BlockSpec((tok, cols), lambda i, ids: (0, 0)),
                pl.BlockSpec((1, cols, blk), lambda i, ids: (where(i), 0, 0)),
            ],
            out_specs=[
                pl.BlockSpec((1, cols, blk), lambda i, ids: (jnp.minimum(i, half - 1), 0, 0)),
                pl.BlockSpec((1, cols, blk), lambda i, ids: (jnp.maximum(i - half, 0), 0, 0)),
            ],
            scratch_shapes=[pltpu.VMEM((cols, tok), BF16)],
        ),
        out_shape=[jax.ShapeDtypeStruct((half, cols, blk), BF16)] * 2,
        compiler_params=params(),
        cost_estimate=cost(2 * tok * cols * blk * count, 2 * count * blk * (tok + 2 * cols)),
        name="weight_keep",
    )(ids, x, g, got)


def last_q_kernel(a_ref, b_ref, out_ref):
    out_ref[...] = (a_ref[0].astype(F32) + b_ref[0].astype(F32)).T


def last_kv_kernel(a_ref, b_ref, out_ref):
    total = a_ref[0].astype(F32) + b_ref[0].astype(F32)
    blk = total.shape[1]
    out_ref[pl.ds(0, blk, 2), :] = total[:HD].T
    out_ref[pl.ds(1, blk, 2), :] = total[HD:].T


def last_q(a, b):
    _, cols, blk = a.shape
    return pl.pallas_call(
        last_q_kernel,
        in_specs=[VSPEC] * 2,
        out_specs=VSPEC,
        out_shape=jax.ShapeDtypeStruct((blk, cols), F32),
        compiler_params=params(),
        cost_estimate=cost(blk * cols, 8 * blk * cols),
        name="last_q",
    )(a, b)


def last_kv(a, b):
    _, cols, blk = a.shape
    out = pl.pallas_call(
        last_kv_kernel,
        in_specs=[VSPEC] * 2,
        out_specs=VSPEC,
        out_shape=jax.ShapeDtypeStruct((2 * blk, HD), F32),
        compiler_params=params(),
        cost_estimate=cost(blk * cols, 8 * blk * cols),
        name="last_kv",
    )(a, b)
    return out.reshape(blk, 2, HD)


def flip(array, axis, bit):
    count = lax.axis_size(axis)
    return lax.ppermute(array, axis, [(i, i ^ (1 << bit)) for i in range(count)])


def doubling(state, axis, levels):
    received = []
    for bit in range(levels):
        got = flip(state, axis, bit)
        received.append(got)
        if bit < levels - 1:
            state = (state.astype(F32) + got.astype(F32)).astype(BF16)
    return received


def weight_grad(x, g, order, seq):
    count = lax.axis_size(seq)
    place = lax.axis_index(seq)
    half = count // 2
    relative = []
    for p in range(half):
        r = 0
        for at, bit in enumerate(order):
            r |= ((p >> (len(order) - 1 - at)) & 1) << bit
        relative.append(r)
    relative = jnp.array(relative, jnp.int32)
    sent = weight_send(place ^ (relative | 1), x, g, half)
    got = flip(sent, seq, 0)
    high, low = weight_keep(place ^ relative, x, g, got, half)
    for at, bit in enumerate(order):
        got = flip(high, seq, bit)
        if at == len(order) - 1:
            return low, got
        total = (low.astype(F32) + got.astype(F32)).astype(BF16)
        size = total.shape[0] // 2
        low, high = total[:size], total[size:]


def body(x, q_weight, kv_weight, norm_gain, out_grad):
    seq, head = "seq", "head"
    levels = (lax.axis_size(seq) - 1).bit_length()
    place = lax.axis_index(seq)
    bits = jnp.stack([(place >> i) & 1 for i in range(levels)]).astype(jnp.int32)
    d = x.shape[1]
    kv, state, wkv = kv_project(x, kv_weight.reshape(2 * d, HD))
    states = doubling(state, seq, levels)
    q, o = q_project(x, q_weight, kv)
    dq, do, own = grad_step(bits, q, o, kv, norm_gain, out_grad, states)
    laters = doubling(own, seq, levels)
    order = list(range(levels - 1, 0, -1))
    q_low, q_got = weight_grad(x, dq, order, seq)
    inner = inner_step(q, do, kv)
    dkv = outer_step(1 - bits, inner, kv, laters)
    kv_low, kv_got = weight_grad(x, dkv, order[::-1], seq)
    partial = jnp.dot(dq, q_weight.T, preferred_element_type=F32)
    partial = partial + jnp.dot(dkv, wkv.T, preferred_element_type=F32)
    input_grad = lax.psum_scatter(partial.astype(BF16), head, scatter_dimension=1, tiled=True)
    return input_grad, last_q(q_low, q_got), last_kv(kv_low, kv_got)


def solution(mesh):
    return jax.shard_map(
        body,
        mesh=mesh,
        in_specs=(
            P("seq", None),
            P(None, "head"),
            P(None, None, "head"),
            P("head"),
            P("seq", "head"),
        ),
        out_specs=(P("seq", "head"), P("seq", "head"), P("seq", None, "head")),
        check_vma=False,
    )
```

time: 231 us -> 138 us (0.60)
  waiting for transfers between devices: 129 us -> 65.5 us
  matrix products: 44.1 us -> 5.76 us
  Pallas kernels: 0 us -> 27.9 us
  blocking collectives: 25.8 us -> 0 us
  starting transfers between devices: 0.08 us -> 11.8 us
  local copies, waits for them, and re-layouts: 15 us -> 12 us
    reduce_scatter x2 -> x1, waiting for transfers between devices: 129 us -> 24.8 us  [body(): lax.psum_scatter(partial.astype(BF16), head, scatter_dimension=1, tiled=T...]
    ppermute x0 -> x12, waiting for transfers between devices: none -> 40.6 us  [flip(): return lax.ppermute(array, axis, [(i, i ^ 1 << bit) for i in range(count)])]
    dot_general x15 -> x2, matrix products: 44.1 us -> 5.76 us  [the longest x1 4.47 us: body(): partial = jnp.dot(dq, q_weight.T, preferred_element_type=F32)]
    pallas_call x0 -> x11, Pallas kernels: none -> 27.9 us  [the longest x2 5.19 us: weight_keep(): pl.pallas_call(functools.partial(keep_kernel, half), grid_spec=pltpu.Pref...]
    all_gather x2 -> x0, blocking collectives: 25.8 us -> none  [the longest x1 13.9 us: entering_2(): lax.all_gather(shard.astype(jnp.bfloat16 if shard.dtype == jnp.float32 el...]
    ppermute x0 -> x12, starting transfers between devices: none -> 11.7 us  [flip(): return lax.ppermute(array, axis, [(i, i ^ 1 << bit) for i in range(count)])]
    slice x4 -> x2, local copies, waits for them, and re-layouts: 7.01 us -> 0.11 us  [weight_grad(): low, high = (total[:size], total[size:])]
    unnamed x34 -> x26, local copies, waits for them, and re-layouts: 6.49 us -> 11.9 us
  transfers between devices with their start and end apart: 2 -> 13, of which waited for: 2 -> 10; matrix products, arithmetic and copies ran while one was open for 5% -> 0% of each run, Pallas kernels for 0% -> 14%
where the time goes in v1:
time: 138 us
  waiting for transfers between devices  65.5 us (47%)
  Pallas kernels  27.9 us (20%)
  between operations  14.3 us (10%)
  local copies, waits for them, and re-layouts  12 us (9%)
  starting transfers between devices  11.8 us (9%)
  matrix products  5.76 us (4%)
    ppermute x12, waiting for transfers between devices, flip(): return lax.ppermute(array, axis, [(i, i ^ 1 << bit) for i in range(count)])  40.6 us
    reduce_scatter x1, waiting for transfers between devices, body(): lax.psum_scatter(partial.astype(BF16), head, scatter_dimension=1, tiled=T...  24.8 us
    unnamed x26, local copies, waits for them, and re-layouts  11.9 us
    ppermute x12, starting transfers between devices, flip(): return lax.ppermute(array, axis, [(i, i ^ 1 << bit) for i in range(count)])  11.7 us
    pallas_call x2, Pallas kernels, weight_keep(): pl.pallas_call(functools.partial(keep_kernel, half), grid_spec=pltpu.Pref...  5.19 us
    pallas_call x1, Pallas kernels, q_project(): pl.pallas_call(q_kernel, grid=(steps,), in_specs=[pl.BlockSpec((tok, blk)...  4.84 us
    pallas_call x2, Pallas kernels, weight_send(): pl.pallas_call(send_kernel, grid_spec=pltpu.PrefetchScalarGridSpec(num_sc...  4.83 us
    dot_general x1, matrix products, body(): partial = jnp.dot(dq, q_weight.T, preferred_element_type=F32)  4.47 us
  transfers between devices with their start and end apart: 13, of which 10 were waited for; matrix products, arithmetic and copies ran while one was open for 0% of the time, Pallas kernels for 14%

profile of v1, /device:TPU:0, one launch (start us, length us, event | category | flops | bytes accessed | tf_op | source)
XLA Modules:
  0.0 137.7 jit_solution(3982519146648509246)
XLA Ops:
  7.2 2.2 %copy-done = bf16[512,4096]{1,0:T(8,128)(2,1)S(1)} copy-done((bf16[512,4096]{1,0:T(8,128)(2,1)S(1)}, bf16[512,4096]{1,0:T(8,128)(2,1)}, u32[]{:S(2)}) %copy-start) | copy-done | bytes 4194328
  9.4 1.6 %copy-done.4 = bf16[4096,2,128]{2,1,0:T(2,128)(2,1)S(1)} copy-done((bf16[4096,2,128]{2,1,0:T(2,128)(2,1)S(1)}, bf16[4096,2,128]{2,1,0:T(2,128)(2,1)}, u32[]{:S(2)}) %copy-start.4) | copy-done | bytes 2097176
  11.0 3.9 %kv_project.1 = (bf16[512,256]{1,0:T(8,128)(2,1)S(1)}, bf16[128,128]{1,0:T(8,128)(2,1)S(1)}, bf16[4096,256]{1,0:T(8,128)(2,1)S(1)}) custom-call(bf16[512,4096]{1,0:T(8,128)(2,1)S(1)} %copy-done, bf16[8192,128]{1,0:T(8,128)(2,1)S(1)} %bitcast.10), custom_call_target="tpu_custom_call" | custom-call | flops 1073741824 | bytes 8388608 | tf_op jit(solution)/shard_map/kv_project/pallas_call | solution.py:74
  16.3 2.9 %collective-permute-start.1 = (bf16[128,128]{1,0:T(8,128)(2,1)S(1)}, bf16[128,128]{1,0:T(8,128)(2,1)S(1)}, u32[]{:S(2)}, u32[]{:S(2)}) collective-permute-start(bf16[128,128]{1,0:T(8,128)(2,1)S(1)} %add_convert_fusion.6), channel_id=1, source_target_pairs={{0,8},{4,12},{8,0},{12,4},{16,24},{20,28},{24,16},{28,20},{1,9},{5... | collective-permute-start | bytes 98312 | tf_op jit(solution)/shard_map/ppermute | solution.py:382
  19.2 4.8 %q_project.1 = (bf16[512,512]{1,0:T(8,128)(2,1)S(1)}, f32[512,512]{1,0:T(8,128)S(1)}) custom-call(bf16[512,4096]{1,0:T(8,128)(2,1)S(1)} %copy-done, bf16[4096,512]{1,0:T(8,128)(2,1)S(1)} %copy-done.2, bf16[512,256]{1,0:T(8,128)(2,1)S(1)} %get-tuple-element.15.kv_ref), custom_call_target="tpu_custom_call" | custom-call | flops 2147483648 | bytes 8388608 | tf_op jit(solution)/shard_map/q_project/pallas_call | solution.py:139
  24.1 1.0 copy-done.5
  25.8 1.6 %collective-permute-start.2 = (bf16[128,128]{1,0:T(8,128)(2,1)S(1)}, bf16[128,128]{1,0:T(8,128)(2,1)S(1)}, u32[]{:S(2)}, u32[]{:S(2)}) collective-permute-start(bf16[128,128]{1,0:T(8,128)(2,1)S(1)} %add_convert_fusion.5), channel_id=1, source_target_pairs={{0,16},{4,20},{8,24},{12,28},{16,0},{20,4},{24,8},{28,12},{1,17},{... | collective-permute-start | bytes 98312 | tf_op jit(solution)/shard_map/ppermute | solution.py:382
  27.5 2.3 %collective-permute-done.2.refs_2_ = bf16[128,128]{1,0:T(8,128)(2,1)S(1)} collective-permute-done((bf16[128,128]{1,0:T(8,128)(2,1)S(1)}, bf16[128,128]{1,0:T(8,128)(2,1)S(1)}, u32[]{:S(2)}, u32[]{:S(2)}) %collective-permute-start.2) | collective-permute-done | bytes 32800 | tf_op jit(solution)/shard_map/ppermute | solution.py:382
  29.8 1.2 copy-done.6
  31.1 1.0 copy-done.7
  32.1 1.0 copy-done.9
  33.1 3.8 %grad_step.1 = (bf16[512,512]{1,0:T(8,128)(2,1)S(1)}, bf16[512,512]{1,0:T(8,128)(2,1)S(1)}, bf16[128,128]{1,0:T(8,128)(2,1)S(1)}) custom-call(s32[3]{0:T(128)S(1)} %get-tuple-element.28.bits_ref, bf16[512,512]{1,0:T(8,128)(2,1)S(1)} %copy-done.9, f32[512,512]{1,0:T(8,128)S(1)} %copy-done.6, bf16[512,256]{1,0:T(8,128)(2,1)S(1)} %get-tuple-element.15.kv_ref, ...), custom_call_target="tpu_custom_call" | custom-call | flops 1073741824 | bytes 3145728 | tf_op jit(solution)/shard_map/grad_step/pallas_call | solution.py:195
  37.0 1.2 collective-permute-done.3.refs_0_
  38.3 3.9 %collective-permute-done.4.refs_1_ = bf16[128,128]{1,0:T(8,128)(2,1)S(1)} collective-permute-done((bf16[128,128]{1,0:T(8,128)(2,1)S(1)}, bf16[128,128]{1,0:T(8,128)(2,1)S(1)}, u32[]{:S(2)}, u32[]{:S(2)}) %collective-permute-start.4) | collective-permute-done | bytes 32800 | tf_op jit(solution)/shard_map/ppermute | solution.py:382
  42.2 1.6 %collective-permute-start.5 = (bf16[128,128]{1,0:T(8,128)(2,1)S(1)}, bf16[128,128]{1,0:T(8,128)(2,1)S(1)}, u32[]{:S(2)}, u32[]{:S(2)}) collective-permute-start(bf16[128,128]{1,0:T(8,128)(2,1)S(1)} %add_convert_fusion.3), channel_id=1, source_target_pairs={{0,16},{4,20},{8,24},{12,28},{16,0},{20,4},{24,8},{28,12},{1,17},{... | collective-permute-start | bytes 98312 | tf_op jit(solution)/shard_map/ppermute | solution.py:382
  43.8 2.2 %inner_step.1.inner_ref = f32[512,256]{1,0:T(8,128)S(1)} custom-call(bf16[512,512]{1,0:T(8,128)(2,1)S(1)} %copy-done.9, bf16[512,512]{1,0:T(8,128)(2,1)S(1)} %get-tuple-element.20.do_ref, bf16[512,256]{1,0:T(8,128)(2,1)S(1)} %get-tuple-element.15.kv_ref), custom_call_target="tpu_custom_call" | custom-call | flops 1073741824 | bytes 2097152 | tf_op jit(solution)/shard_map/inner_step/pallas_call | solution.py:231
  47.0 1.3 fusion.3
  49.2 4.5 %add_convert_fusion = bf16[512,4096]{1,0:T(8,128)(2,1)} fusion(f32[512,4096]{1,0:T(8,128)S(1)} %fusion.3, bf16[512,512]{1,0:T(8,128)(2,1)S(1)} %get-tuple-element.19.g_ref, bf16[4096,512]{1,0:T(8,128)(2,1)S(1)} %copy-done.3), kind=kOutput, calls=%fused_computation | convolution fusion | flops 2151677952 | bytes 17301504 | tf_op jit(solution)/shard_map/dot_general | solution.py:434
  53.7 2.2 %copy-done.1 = bf16[512,4096]{1,0:T(8,128)(2,1)S(1)} copy-done((bf16[512,4096]{1,0:T(8,128)(2,1)S(1)}, bf16[512,4096]{1,0:T(8,128)(2,1)}, u32[]{:S(2)}) %copy-start.1) | copy-done | bytes 4194328
  55.9 2.7 %weight_send.2 = bf16[4,512,512]{2,1,0:T(8,128)(2,1)S(1)} custom-call(s32[4]{0:T(128)S(1)} %or_xor_fusion.ids_ref, bf16[512,4096]{1,0:T(8,128)(2,1)S(1)} %copy-done.1, bf16[512,512]{1,0:T(8,128)(2,1)S(1)} %get-tuple-element.19.g_ref), custom_call_target="tpu_custom_call" | custom-call | flops 1073741824 | bytes 4194304 | tf_op jit(solution)/shard_map/weight_send/pallas_call | solution.py:276
  58.7 2.1 %weight_send.3 = bf16[4,256,512]{2,1,0:T(8,128)(2,1)S(1)} custom-call(s32[4]{0:T(128)S(1)} %broadcast_xor_fusion.ids_ref, bf16[512,4096]{1,0:T(8,128)(2,1)S(1)} %copy-done.1, bf16[512,256]{1,0:T(8,128)(2,1)S(1)} %outer_step.1.g_ref), custom_call_target="tpu_custom_call" | custom-call | flops 536870912 | bytes 3145728 | tf_op jit(solution)/shard_map/weight_send/pallas_call | solution.py:276
  61.4 1.4 %collective-permute-done.6.got_ref = bf16[4,512,512]{2,1,0:T(8,128)(2,1)S(1)} collective-permute-done((bf16[4,512,512]{2,1,0:T(8,128)(2,1)S(1)}, bf16[4,512,512]{2,1,0:T(8,128)(2,1)S(1)}, u32[]{:S(2)}, u32[]{:S(2)}) %collective-permute-start.6) | collective-permute-done | bytes 2097184 | tf_op jit(solution)/shard_map/ppermute | solution.py:382
  62.8 3.0 %weight_keep.2 = (bf16[2,512,512]{2,1,0:T(8,128)(2,1)S(1)}, bf16[2,512,512]{2,1,0:T(8,128)(2,1)S(1)}) custom-call(s32[4]{0:T(128)S(1)} %fusion.ids_ref, bf16[512,4096]{1,0:T(8,128)(2,1)S(1)} %copy-done.1, bf16[512,512]{1,0:T(8,128)(2,1)S(1)} %get-tuple-element.19.g_ref, bf16[4,512,512]{2,1,0:T(8,128)(2,1)S(1)} %collective-permute-done.6.got_ref), custom_call_target="tpu_custom_call" | custom-call | flops 1073741824 | bytes 6291456 | tf_op jit(solution)/shard_map/weight_keep/pallas_call | solution.py:319
  65.8 1.6 %collective-permute-start.7 = (bf16[2,512,512]{2,1,0:T(8,128)(2,1)S(1)}, bf16[2,512,512]{2,1,0:T(8,128)(2,1)S(1)}, u32[]{:S(2)}, u32[]{:S(2)}) collective-permute-start(bf16[2,512,512]{2,1,0:T(8,128)(2,1)S(1)} %get-tuple-element.24), channel_id=1, source_target_pairs={{0,16},{4,20},{8,24},{12,28},{16,0},{20,4},{24,8},{28,12},{1,17},{... | collective-permute-start | bytes 3145736 | tf_op jit(solution)/shard_map/ppermute | solution.py:382
  67.4 2.2 %weight_keep.3 = (bf16[2,256,512]{2,1,0:T(8,128)(2,1)S(1)}, bf16[2,256,512]{2,1,0:T(8,128)(2,1)S(1)}) custom-call(s32[4]{0:T(128)S(1)} %broadcast_xor_fusion.1.ids_ref, bf16[512,4096]{1,0:T(8,128)(2,1)S(1)} %copy-done.1, bf16[512,256]{1,0:T(8,128)(2,1)S(1)} %outer_step.1.g_ref, bf16[4,256,512]{2,1,0:T(8,128)(2,1)S(1)} %collective-permute-done.9.got_ref), custom_call_target="tpu_custom_call" | custom-call | flops 536870912 | bytes 4194304 | tf_op jit(solution)/shard_map/weight_keep/pallas_call | solution.py:319
  70.2 20.8 %collective-permute-done.7 = bf16[2,512,512]{2,1,0:T(8,128)(2,1)S(1)} collective-permute-done((bf16[2,512,512]{2,1,0:T(8,128)(2,1)S(1)}, bf16[2,512,512]{2,1,0:T(8,128)(2,1)S(1)}, u32[]{:S(2)}, u32[]{:S(2)}) %collective-permute-start.7) | collective-permute-done | bytes 1048608 | tf_op jit(solution)/shard_map/ppermute | solution.py:382
  92.1 1.7 %collective-permute-start.11 = (bf16[1,256,512]{2,1,0:T(8,128)(2,1)S(1)}, bf16[1,256,512]{2,1,0:T(8,128)(2,1)S(1)}, u32[]{:S(2)}, u32[]{:S(2)}) collective-permute-start(bf16[1,256,512]{2,1,0:T(8,128)(2,1)S(1)} %get-tuple-element.31), channel_id=1, source_target_pairs={{0,16},{4,20},{8,24},{12,28},{16,0},{20,4},{24,8},{28,12},{1,17},{... | collective-permute-start | bytes 786440 | tf_op jit(solution)/shard_map/ppermute | solution.py:382
  93.8 5.7 %collective-permute-done.11.b_ref = bf16[1,256,512]{2,1,0:T(8,128)(2,1)S(1)} collective-permute-done((bf16[1,256,512]{2,1,0:T(8,128)(2,1)S(1)}, bf16[1,256,512]{2,1,0:T(8,128)(2,1)S(1)}, u32[]{:S(2)}, u32[]{:S(2)}) %collective-permute-start.11) | collective-permute-done | bytes 262176 | tf_op jit(solution)/shard_map/ppermute | solution.py:382
  99.5 1.0 last_kv.1
  100.5 4.3 %collective-permute-done.8.b_ref = bf16[1,512,512]{2,1,0:T(8,128)(2,1)S(1)} collective-permute-done((bf16[1,512,512]{2,1,0:T(8,128)(2,1)S(1)}, bf16[1,512,512]{2,1,0:T(8,128)(2,1)S(1)}, u32[]{:S(2)}, u32[]{:S(2)}) %collective-permute-start.8) | collective-permute-done | bytes 524320 | tf_op jit(solution)/shard_map/ppermute | solution.py:382
  104.8 1.3 last_q.1
  106.1 24.8 %reduce-scatter.2.cloned.1.call-done = bf16[512,1024]{1,0:T(8,128)(2,1)} async-done(((bf16[512,4096]{1,0:T(8,128)(2,1)}), bf16[512,1024]{1,0:T(8,128)(2,1)}) %reduce-scatter.2.cloned.1.call-update) | async-done | bytes 1048592 | tf_op jit(solution)/shard_map/reduce_scatter | solution.py:436
  (47 shorter events, 6.6 us)
Async XLA Ops:
  7.2 123.7 %reduce-scatter.2.cloned.1.call-start = ((), (), s32[]{:S(2)}) async-start(), calls=%async_computation.1 | async-start | bytes 5242880 | tf_op jit(solution)/shard_map/reduce_scatter | solution.py:436
  7.2 2.2 %copy-start = (bf16[512,4096]{1,0:T(8,128)(2,1)S(1)}, bf16[512,4096]{1,0:T(8,128)(2,1)}, u32[]{:S(2)}) copy-start(bf16[512,4096]{1,0:T(8,128)(2,1)} %x_ref.11) | copy-start | bytes 12582916
  9.4 1.6 %copy-start.4 = (bf16[4096,2,128]{2,1,0:T(2,128)(2,1)S(1)}, bf16[4096,2,128]{2,1,0:T(2,128)(2,1)}, u32[]{:S(2)}) copy-start(bf16[4096,2,128]{2,1,0:T(2,128)(2,1)} %param.9) | copy-start | bytes 6291460
  11.0 8.2 %copy-start.2 = (bf16[4096,512]{1,0:T(8,128)(2,1)S(1)}, bf16[4096,512]{1,0:T(8,128)(2,1)}, u32[]{:S(2)}) copy-start(bf16[4096,512]{1,0:T(8,128)(2,1)} %w_ref.1) | copy-start | bytes 12582916
  14.9 1.4 %collective-permute-start = (bf16[128,128]{1,0:T(8,128)(2,1)S(1)}, bf16[128,128]{1,0:T(8,128)(2,1)S(1)}, u32[]{:S(2)}, u32[]{:S(2)}) collective-permute-start(bf16[128,128]{1,0:T(8,128)(2,1)S(1)} %get-tuple-element.18), channel_id=1, source_target_pairs={{0,4},{4,0},{8,12},{12,8},{16,20},{20,16},{24,28},{28,24},{1,5},{5... | collective-permute-start | bytes 98312 | tf_op jit(solution)/shard_map/ppermute | solution.py:382
  16.3 9.5 %collective-permute-start.1 = (bf16[128,128]{1,0:T(8,128)(2,1)S(1)}, bf16[128,128]{1,0:T(8,128)(2,1)S(1)}, u32[]{:S(2)}, u32[]{:S(2)}) collective-permute-start(bf16[128,128]{1,0:T(8,128)(2,1)S(1)} %add_convert_fusion.6), channel_id=1, source_target_pairs={{0,8},{4,12},{8,0},{12,4},{16,24},{20,28},{24,16},{28,20},{1,9},{5... | collective-permute-start | bytes 98312 | tf_op jit(solution)/shard_map/ppermute | solution.py:382
  19.2 10.6 %copy-start.10 = (f32[512]{0:T(512)S(1)}, f32[512]{0:T(512)}, u32[]{:S(2)}) copy-start(f32[512]{0:T(512)} %param.10) | copy-start | bytes 6148
  24.1 1.0 copy-start.5
  25.0 0.8 copy-start.8
  25.8 4.0 %collective-permute-start.2 = (bf16[128,128]{1,0:T(8,128)(2,1)S(1)}, bf16[128,128]{1,0:T(8,128)(2,1)S(1)}, u32[]{:S(2)}, u32[]{:S(2)}) collective-permute-start(bf16[128,128]{1,0:T(8,128)(2,1)S(1)} %add_convert_fusion.5), channel_id=1, source_target_pairs={{0,16},{4,20},{8,24},{12,28},{16,0},{20,4},{24,8},{28,12},{1,17},{... | collective-permute-start | bytes 98312 | tf_op jit(solution)/shard_map/ppermute | solution.py:382
  29.8 1.2 copy-start.6
  31.1 1.0 copy-start.7
  32.1 1.0 copy-start.9
  36.9 1.3 collective-permute-start.3
  38.2 4.0 %collective-permute-start.4 = (bf16[128,128]{1,0:T(8,128)(2,1)S(1)}, bf16[128,128]{1,0:T(8,128)(2,1)S(1)}, u32[]{:S(2)}, u32[]{:S(2)}) collective-permute-start(bf16[128,128]{1,0:T(8,128)(2,1)S(1)} %add_convert_fusion.4), channel_id=1, source_target_pairs={{0,8},{4,12},{8,0},{12,4},{16,24},{20,28},{24,16},{28,20},{1,9},{5... | collective-permute-start | bytes 98312 | tf_op jit(solution)/shard_map/ppermute | solution.py:382
  42.2 4.0 %collective-permute-start.5 = (bf16[128,128]{1,0:T(8,128)(2,1)S(1)}, bf16[128,128]{1,0:T(8,128)(2,1)S(1)}, u32[]{:S(2)}, u32[]{:S(2)}) collective-permute-start(bf16[128,128]{1,0:T(8,128)(2,1)S(1)} %add_convert_fusion.3), channel_id=1, source_target_pairs={{0,16},{4,20},{8,24},{12,28},{16,0},{20,4},{24,8},{28,12},{1,17},{... | collective-permute-start | bytes 98312 | tf_op jit(solution)/shard_map/ppermute | solution.py:382
  47.0 2.2 %copy-start.3 = (bf16[4096,512]{1,0:T(8,128)(2,1)S(1)}, bf16[4096,512]{1,0:T(8,128)(2,1)}, u32[]{:S(2)}) copy-start(bf16[4096,512]{1,0:T(8,128)(2,1)} %w_ref.1) | copy-start | bytes 12582916
  53.7 5.0 %copy-start.12 = (s32[4]{0:T(128)S(1)}, s32[4]{0:T(128)}, u32[]{:S(2)}) copy-start(s32[4]{0:T(128)} %constant.21) | copy-start | bytes 52
  53.7 2.2 %copy-start.1 = (bf16[512,4096]{1,0:T(8,128)(2,1)S(1)}, bf16[512,4096]{1,0:T(8,128)(2,1)}, u32[]{:S(2)}) copy-start(bf16[512,4096]{1,0:T(8,128)(2,1)} %x_ref.11) | copy-start | bytes 12582916
  58.6 4.2 %collective-permute-start.6 = (bf16[4,512,512]{2,1,0:T(8,128)(2,1)S(1)}, bf16[4,512,512]{2,1,0:T(8,128)(2,1)S(1)}, u32[]{:S(2)}, u32[]{:S(2)}) collective-permute-start(bf16[4,512,512]{2,1,0:T(8,128)(2,1)S(1)} %weight_send.2), channel_id=1, source_target_pairs={{0,4},{4,0},{8,12},{12,8},{16,20},{20,16},{24,28},{28,24},{1,5},{5... | collective-permute-start | bytes 6291464 | tf_op jit(solution)/shard_map/ppermute | solution.py:382
  60.8 6.5 %copy-start.11 = (s32[4]{0:T(128)S(1)}, s32[4]{0:T(128)}, u32[]{:S(2)}) copy-start(s32[4]{0:T(128)} %constant.20.clone) | copy-start | bytes 52
  60.9 6.5 %collective-permute-start.9 = (bf16[4,256,512]{2,1,0:T(8,128)(2,1)S(1)}, bf16[4,256,512]{2,1,0:T(8,128)(2,1)S(1)}, u32[]{:S(2)}, u32[]{:S(2)}) collective-permute-start(bf16[4,256,512]{2,1,0:T(8,128)(2,1)S(1)} %weight_send.3), channel_id=1, source_target_pairs={{0,4},{4,0},{8,12},{12,8},{16,20},{20,16},{24,28},{28,24},{1,5},{5... | collective-permute-start | bytes 3145736 | tf_op jit(solution)/shard_map/ppermute | solution.py:382
  65.8 25.3 %collective-permute-start.7 = (bf16[2,512,512]{2,1,0:T(8,128)(2,1)S(1)}, bf16[2,512,512]{2,1,0:T(8,128)(2,1)S(1)}, u32[]{:S(2)}, u32[]{:S(2)}) collective-permute-start(bf16[2,512,512]{2,1,0:T(8,128)(2,1)S(1)} %get-tuple-element.24), channel_id=1, source_target_pairs={{0,16},{4,20},{8,24},{12,28},{16,0},{20,4},{24,8},{28,12},{1,17},{... | collective-permute-start | bytes 3145736 | tf_op jit(solution)/shard_map/ppermute | solution.py:382
  69.6 22.3 %collective-permute-start.10 = (bf16[2,256,512]{2,1,0:T(8,128)(2,1)S(1)}, bf16[2,256,512]{2,1,0:T(8,128)(2,1)S(1)}, u32[]{:S(2)}, u32[]{:S(2)}) collective-permute-start(bf16[2,256,512]{2,1,0:T(8,128)(2,1)S(1)} %get-tuple-element.26), channel_id=1, source_target_pairs={{0,8},{4,12},{8,0},{12,4},{16,24},{20,28},{24,16},{28,20},{1,9},{5... | collective-permute-start | bytes 1572872 | tf_op jit(solution)/shard_map/ppermute | solution.py:382
  91.5 13.3 %collective-permute-start.8 = (bf16[1,512,512]{2,1,0:T(8,128)(2,1)S(1)}, bf16[1,512,512]{2,1,0:T(8,128)(2,1)S(1)}, u32[]{:S(2)}, u32[]{:S(2)}) collective-permute-start(bf16[1,512,512]{2,1,0:T(8,128)(2,1)S(1)} %get-tuple-element.29), channel_id=1, source_target_pairs={{0,8},{4,12},{8,0},{12,4},{16,24},{20,28},{24,16},{28,20},{1,9},{5... | collective-permute-start | bytes 1572872 | tf_op jit(solution)/shard_map/ppermute | solution.py:382
  92.1 7.4 %collective-permute-start.11 = (bf16[1,256,512]{2,1,0:T(8,128)(2,1)S(1)}, bf16[1,256,512]{2,1,0:T(8,128)(2,1)S(1)}, u32[]{:S(2)}, u32[]{:S(2)}) collective-permute-start(bf16[1,256,512]{2,1,0:T(8,128)(2,1)S(1)} %get-tuple-element.31), channel_id=1, source_target_pairs={{0,16},{4,20},{8,24},{12,28},{16,0},{20,4},{24,8},{28,12},{1,17},{... | collective-permute-start | bytes 786440 | tf_op jit(solution)/shard_map/ppermute | solution.py:382
Sparse Core Ops, SparseCore 0:
  53.8 77.0 reduce-scatter.1

commit v2 on v1

v2 whole, which is shorter than its diff:
```python
import functools

import jax
import jax.numpy as jnp
from jax import lax
from jax.experimental import pallas as pl
from jax.experimental.pallas import tpu as pltpu
from jax.sharding import PartitionSpec as P

HD = 128
PARTS = 2
EPSILON = 1e-05
F32 = jnp.float32
BF16 = jnp.bfloat16
VMEM_LIMIT = 18 * 1024 * 1024
VMEM_MOST = 58 * 1024 * 1024


def mm(a, b):
    return jnp.dot(a, b, preferred_element_type=F32)


def mm_nt(a, b):
    return lax.dot_general(a, b, (((1,), (1,)), ((), ())), preferred_element_type=F32)


def mm_tn(a, b):
    return lax.dot_general(a, b, (((0,), (0,)), ((), ())), preferred_element_type=F32)


def params(limit):
    return pltpu.CompilerParams(vmem_limit_bytes=limit)


def cost(flops, nbytes):
    return pl.CostEstimate(
        flops=int(flops) // 64, bytes_accessed=int(nbytes) // 64, transcendentals=0
    )


def ordered(kernel, after, args, *, in_specs, lead=0, grid=None, out_specs, scratch=(), limit=VMEM_LIMIT, **kw):
    given = len(args) - lead
    extra = len(after)

    def run(*refs):
        kernel(*refs[: lead + given], *refs[lead + given + extra :])

    in_specs = list(in_specs) + [pl.BlockSpec(memory_space=pl.ANY)] * extra
    return pl.pallas_call(
        run,
        grid_spec=pltpu.PrefetchScalarGridSpec(
            num_scalar_prefetch=lead,
            grid=grid or (),
            in_specs=in_specs,
            out_specs=out_specs,
            scratch_shapes=scratch,
        ),
        compiler_params=params(limit),
        **kw,
    )(*args, *after)


ANY = pl.BlockSpec(memory_space=pl.ANY)
VSPEC = pl.BlockSpec(memory_space=pltpu.VMEM)
SSPEC = pl.BlockSpec(memory_space=pltpu.SMEM)


def parting(rows):
    half = rows // 2
    row = lax.broadcasted_iota(jnp.int32, (rows, rows), 0)
    col = lax.broadcasted_iota(jnp.int32, (rows, rows), 1)
    target = jnp.where(row < half, 2 * row, 2 * (row - half) + 1)
    return jnp.where(col == target, 1.0, 0.0).astype(BF16)


def kv_kernel(x_ref, w_ref, kv_ref, state_ref, wkv_ref, acc_ref):
    step = pl.program_id(0)
    steps = pl.num_programs(0)
    rows = 2 * HD
    perm = parting(rows)
    for i in range(w_ref.shape[0] // rows):
        both = mm(perm, w_ref[i * rows : (i + 1) * rows, :]).astype(BF16)
        wkv_ref[i * HD : (i + 1) * HD, :HD] = both[:HD]
        wkv_ref[i * HD : (i + 1) * HD, HD:] = both[HD:]
    part = mm(x_ref[...], wkv_ref[...])

    @pl.when(step == 0)
    def _():
        acc_ref[...] = part

    @pl.when(step > 0)
    def _():
        acc_ref[...] += part

    @pl.when(step == steps - 1)
    def _():
        kv = acc_ref[...].astype(BF16)
        kv_ref[...] = kv
        state_ref[...] = mm_tn(kv[:, :HD], kv[:, HD:]).astype(BF16)


def kv_project(x, kv_flat, after=()):
    tok, d = x.shape
    steps = 4
    blk = d // steps
    return ordered(
        kv_kernel,
        after,
        (x, kv_flat),
        grid=(steps,),
        in_specs=[
            pl.BlockSpec((tok, blk), lambda i: (0, i)),
            pl.BlockSpec((2 * blk, HD), lambda i: (i, 0)),
        ],
        out_specs=[
            pl.BlockSpec((tok, 2 * HD), lambda i: (0, 0)),
            pl.BlockSpec((HD, HD), lambda i: (0, 0)),
            pl.BlockSpec((blk, 2 * HD), lambda i: (i, 0)),
        ],
        out_shape=[
            jax.ShapeDtypeStruct((tok, 2 * HD), BF16),
            jax.ShapeDtypeStruct((HD, HD), BF16),
            jax.ShapeDtypeStruct((d, 2 * HD), BF16),
        ],
        scratch=[pltpu.VMEM((tok, 2 * HD), F32)],
        cost_estimate=cost(4 * tok * d * HD, 2 * (tok * d + 4 * d * HD)),
        name="kv_project",
    )


def halves(tok):
    blk = min(256, tok)
    return [(lo, lo + blk) for lo in range(0, tok, blk)]


def masked(scores, row_first):
    rows, cols = scores.shape
    row = lax.broadcasted_iota(jnp.int32, (rows, cols), 0) + row_first
    col = lax.broadcasted_iota(jnp.int32, (rows, cols), 1)
    return jnp.where(col <= row, scores, 0.0)


def q_kernel(x_ref, w_ref, q_ref, acc_ref):
    step = pl.program_id(0)
    steps = pl.num_programs(0)
    part = mm(x_ref[...], w_ref[...])

    @pl.when(step == 0)
    def _():
        acc_ref[...] = part

    @pl.when((step > 0) & (step < steps - 1))
    def _():
        acc_ref[...] += part

    @pl.when(step == steps - 1)
    def _():
        q_ref[...] = (acc_ref[...] + part).astype(BF16)


def q_project(x, q_weight, after=()):
    tok, d = x.shape
    cols = q_weight.shape[1]
    steps = 4
    blk = d // steps
    return ordered(
        q_kernel,
        after,
        (x, q_weight),
        grid=(steps,),
        in_specs=[
            pl.BlockSpec((tok, blk), lambda i: (0, i)),
            pl.BlockSpec((blk, cols), lambda i: (i, 0)),
        ],
        out_specs=pl.BlockSpec((tok, cols), lambda i: (0, 0)),
        out_shape=jax.ShapeDtypeStruct((tok, cols), BF16),
        scratch=[pltpu.VMEM((tok, cols), F32)],
        cost_estimate=cost(2 * tok * d * cols, 2 * (tok * d + d * cols)),
        name="q_project",
    )


def intra_kernel(q_ref, kv_ref, o_ref):
    k, v = kv_ref[:, :HD], kv_ref[:, HD:]
    for lo, hi in halves(q_ref.shape[0]):
        for h in range(q_ref.shape[1] // HD):
            c = slice(h * HD, (h + 1) * HD)
            s = masked(mm_nt(q_ref[lo:hi, c], k[:hi]), lo)
            o_ref[lo:hi, c] = mm(s.astype(BF16), v[:hi])


def intra(q, kv, after=()):
    tok, cols = q.shape
    return ordered(
        intra_kernel,
        after,
        (q, kv),
        in_specs=[VSPEC] * 2,
        out_specs=VSPEC,
        out_shape=jax.ShapeDtypeStruct((tok, cols), F32),
        cost_estimate=cost(4 * tok * tok * cols, 6 * tok * cols),
        name="intra",
    )


def weighted(bits_ref, refs):
    total = None
    for i, ref in enumerate(refs):
        term = ref[...].astype(F32) * bits_ref[i].astype(F32)
        total = term if total is None else total + term
    return total


def grad_kernel(n, bits_ref, q_ref, o_ref, kv_ref, gain_ref, up_ref, *refs):
    states, (dq_ref, do_ref, own_ref) = refs[:n], refs[n:]
    prev = weighted(bits_ref, states).astype(BF16)
    k, v = kv_ref[:, :HD], kv_ref[:, HD:]
    own = None
    for lo, hi in halves(q_ref.shape[0]):
        for h in range(q_ref.shape[1] // HD):
            c = slice(h * HD, (h + 1) * HD)
            q = q_ref[lo:hi, c]
            o = o_ref[lo:hi, c] + mm(q, prev)
            inv = lax.rsqrt(jnp.mean(o * o, axis=-1, keepdims=True) + EPSILON)
            scaled = gain_ref[:, c] * up_ref[lo:hi, c].astype(F32)
            along = jnp.mean(scaled * o, axis=-1, keepdims=True)
            do = (inv * (scaled - o * ((inv * inv) * along))).astype(BF16)
            do_ref[lo:hi, c] = do
            s = masked(mm_nt(do, v[:hi]), lo).astype(BF16)
            dq_ref[c, lo:hi] = (mm(s, k[:hi]) + mm_nt(do, prev)).T.astype(BF16)
            part = mm_tn(q, do)
            own = part if own is None else own + part
    own_ref[...] = own.astype(BF16)


def grad_step(bits, q, o, kv, gain, upstream, states, after=()):
    tok, cols = q.shape
    n = len(states)
    return ordered(
        functools.partial(grad_kernel, n),
        after,
        (bits, q, o, kv, gain.reshape(1, cols), upstream, *states),
        in_specs=[SSPEC] + [VSPEC] * (5 + n),
        out_specs=[VSPEC] * 3,
        out_shape=[
            jax.ShapeDtypeStruct((cols, tok), BF16),
            jax.ShapeDtypeStruct((tok, cols), BF16),
            jax.ShapeDtypeStruct((HD, HD), BF16),
        ],
        cost_estimate=cost(8 * tok * tok * cols, 12 * tok * cols),
        name="grad_step",
    )


def inner_kernel(q_ref, do_ref, kv_ref, out_ref):
    k, v = kv_ref[:, :HD], kv_ref[:, HD:]
    tok = q_ref.shape[0]
    for lo, hi in halves(tok):
        col = lax.broadcasted_iota(jnp.int32, (hi - lo, tok - lo), 1)
        row = lax.broadcasted_iota(jnp.int32, (hi - lo, tok - lo), 0)
        dk = dv = None
        for h in range(q_ref.shape[1] // HD):
            c = slice(h * HD, (h + 1) * HD)
            q, do = q_ref[lo:, c], do_ref[lo:, c]
            s = jnp.where(col >= row, mm_nt(k[lo:hi], q), 0.0).astype(BF16)
            ds = jnp.where(col >= row, mm_nt(v[lo:hi], do), 0.0).astype(BF16)
            dk_h, dv_h = mm(ds, q), mm(s, do)
            dk = dk_h if dk is None else dk + dk_h
            dv = dv_h if dv is None else dv + dv_h
        out_ref[lo:hi, :HD] = dk
        out_ref[lo:hi, HD:] = dv


def inner_step(q, do, kv, after=()):
    tok, cols = q.shape
    return ordered(
        inner_kernel,
        after,
        (q, do, kv),
        in_specs=[VSPEC] * 3,
        out_specs=VSPEC,
        out_shape=jax.ShapeDtypeStruct((tok, 2 * HD), F32),
        cost_estimate=cost(8 * tok * tok * cols, 8 * tok * cols),
        name="inner_step",
    )


def outer_kernel(n, bits_ref, inner_ref, kv_ref, dq_ref, *refs):
    states, out_ref = refs[:n], refs[n]
    later = weighted(bits_ref, states).astype(BF16)
    k, v = kv_ref[:, :HD], kv_ref[:, HD:]
    cols = dq_ref.shape[0]
    out_ref[:cols, :] = dq_ref[...]
    out_ref[cols : cols + HD, :] = (inner_ref[:, :HD] + mm_nt(v, later)).T.astype(BF16)
    out_ref[cols + HD :, :] = (inner_ref[:, HD:] + mm(k, later)).T.astype(BF16)


def outer_step(bits, inner, kv, dq, states, after=()):
    tok = kv.shape[0]
    width = dq.shape[0] + 2 * HD
    n = len(states)
    return ordered(
        functools.partial(outer_kernel, n),
        after,
        (bits, inner, kv, dq, *states),
        in_specs=[SSPEC] + [VSPEC] * (3 + n),
        out_specs=VSPEC,
        out_shape=jax.ShapeDtypeStruct((width, tok), BF16),
        cost_estimate=cost(4 * tok * HD * HD, 8 * tok * HD),
        name="outer_step",
    )


def send_kernel(ids_ref, x_ref, g_ref, out_ref):
    out_ref[0] = mm(g_ref[...], x_ref[...]).astype(BF16)


def keep_kernel(half, ids_ref, x_ref, g_ref, got_ref, high_ref, low_ref):
    total = (mm(g_ref[...], x_ref[...]) + got_ref[0].astype(F32)).astype(BF16)

    @pl.when(pl.program_id(0) < half)
    def _():
        high_ref[0] = total

    @pl.when(pl.program_id(0) >= half)
    def _():
        low_ref[0] = total


def weight_keep(x, g, got, seq, after=()):
    tok, d = x.shape
    cols = g.shape[0]
    count = lax.axis_size(seq) // 2
    half = count // 2
    blk = d // (2 * count)
    order = [(i + half) % count for i in range(count)]
    ids = jnp.stack([lax.axis_index(seq) ^ (2 * i) for i in order]).astype(jnp.int32)
    return ordered(
        functools.partial(keep_kernel, half),
        after,
        (ids, x, g, got),
        lead=1,
        grid=(count,),
        in_specs=[
            pl.BlockSpec((tok, blk), lambda i, ids: (0, ids[i])),
            pl.BlockSpec((cols, tok), lambda i, ids: (0, 0)),
            pl.BlockSpec((1, cols, blk), lambda i, ids: (lax.shift_right_logical(ids[i], 1), 0, 0)),
        ],
        out_specs=[
            pl.BlockSpec((1, cols, blk), lambda i, ids: (jnp.minimum(i, half - 1), 0, 0)),
            pl.BlockSpec((1, cols, blk), lambda i, ids: (jnp.maximum(i - half, 0), 0, 0)),
        ],
        out_shape=[jax.ShapeDtypeStruct((half, cols, blk), BF16)] * 2,
        cost_estimate=cost(2 * tok * cols * blk * count, 2 * count * blk * (tok + 2 * cols)),
        name="weight_keep",
    )


def fold_kernel(a_ref, b_ref, high_ref, low_ref):
    half = a_ref.shape[0] // 2
    total = (a_ref[...].astype(F32) + b_ref[...].astype(F32)).astype(BF16)
    low_ref[...] = total[:half]
    high_ref[...] = total[half:]


def fold(a, b):
    m, cols, blk = a.shape
    return ordered(
        fold_kernel,
        (),
        (a, b),
        in_specs=[VSPEC] * 2,
        out_specs=[VSPEC] * 2,
        out_shape=[jax.ShapeDtypeStruct((m // 2, cols, blk), BF16)] * 2,
        cost_estimate=cost(a.size, 6 * a.size),
        name="fold",
    )


def weight_send(parity, x, g, seq, after=()):
    tok, d = x.shape
    cols = g.shape[0]
    count = lax.axis_size(seq) // 2
    blk = d // (2 * count)
    return ordered(
        send_kernel,
        after,
        (parity, x, g),
        lead=1,
        grid=(count,),
        in_specs=[
            pl.BlockSpec((tok, blk), lambda i, ids: (0, 2 * i + ids[0])),
            pl.BlockSpec((cols, tok), lambda i, ids: (0, 0)),
        ],
        out_specs=pl.BlockSpec((1, cols, blk), lambda i, ids: (i, 0, 0)),
        out_shape=jax.ShapeDtypeStruct((count, cols, blk), BF16),
        cost_estimate=cost(2 * tok * cols * blk * count, 2 * count * blk * (tok + cols)),
        name="weight_send",
    )


def last_kernel(*refs):
    q_ref, kv_ref = refs[-2:]
    total = refs[0][0].astype(F32)
    for ref in refs[1:-2]:
        total = total + ref[0].astype(F32)
    blk, cols = q_ref.shape
    q_ref[...] = total[:cols].T
    kv_ref[pl.ds(0, blk, 2), :] = total[cols : cols + HD].T
    kv_ref[pl.ds(1, blk, 2), :] = total[cols + HD :].T


def weight_last(parts, after=()):
    _, width, blk = parts[0].shape
    cols = width - 2 * HD
    q, kv = ordered(
        last_kernel,
        after,
        tuple(parts),
        in_specs=[VSPEC] * len(parts),
        out_specs=[VSPEC] * 2,
        out_shape=[
            jax.ShapeDtypeStruct((blk, cols), F32),
            jax.ShapeDtypeStruct((2 * blk, HD), F32),
        ],
        cost_estimate=cost(blk * cols, 8 * blk * cols),
        name="weight_last",
    )
    return q, kv.reshape(blk, 2, HD)


def flip(array, axis, bit):
    count = lax.axis_size(axis)
    return lax.ppermute(array, axis, [(i, i ^ (1 << bit)) for i in range(count)])


def merge_kernel(a_ref, b_ref, out_ref):
    out_ref[...] = (a_ref[...].astype(F32) + b_ref[...].astype(F32)).astype(BF16)


def merge(a, b, after=()):
    return ordered(
        merge_kernel,
        after,
        (a, b),
        in_specs=[VSPEC] * 2,
        out_specs=VSPEC,
        out_shape=jax.ShapeDtypeStruct(a.shape, BF16),
        cost_estimate=cost(a.size, 6 * a.size),
        name="merge",
    )


def doubling(state, axis, levels, between):
    received = []
    done = None
    for bit in range(levels):
        got = flip(state, axis, bit)
        received.append(got)
        if bit == 0:
            done = between(got)
        if bit < levels - 1:
            state = merge(state, got, after=() if bit == 0 else (done,))
    return received, done


def partial_kernel(ids_ref, q_ref, kv_ref, g_ref, *refs):
    cols = q_ref.shape[1]
    total = mm(q_ref[...], g_ref[:cols, :]) + mm(kv_ref[...], g_ref[cols:, :])
    for ref in refs[:-1]:
        total = total + ref[...].astype(F32)
    refs[-1][...] = total.astype(BF16)


def partial(at, part, parts, ids, q_weight, wkv, grads, got, n, after=()):
    d, cols = q_weight.shape
    width, tok = grads.shape
    rows, some = d // n, tok // parts
    steps = 2
    tile = rows // steps
    out = pl.BlockSpec((tile, some), lambda i, ids: (i, 0))
    return ordered(
        partial_kernel,
        after,
        (ids, q_weight, wkv, grads, *got),
        lead=1,
        grid=(steps,),
        in_specs=[
            pl.BlockSpec((tile, cols), lambda i, ids: (ids[at] * steps + i, 0)),
            pl.BlockSpec((tile, width - cols), lambda i, ids: (ids[at] * steps + i, 0)),
            pl.BlockSpec((width, some), lambda i, ids: (0, part)),
        ]
        + [out] * len(got),
        out_specs=out,
        out_shape=jax.ShapeDtypeStruct((rows, some), BF16),
        cost_estimate=cost(2 * rows * width * some, 2 * rows * (width + 2 * some)),
        name="partial",
    )


def final_kernel(parts, *refs):
    out_ref = refs[-1]
    each = (len(refs) - 1) // parts
    some = out_ref.shape[0] // parts
    for part in range(parts):
        total = None
        for ref in refs[part * each : (part + 1) * each]:
            term = ref[...].astype(F32)
            total = term if total is None else total + term
        out_ref[part * some : (part + 1) * some, :] = total.T.astype(BF16)


def final(groups, after=()):
    arrays = [array for group in groups for array in group]
    rows, some = arrays[0].shape
    tok = some * len(groups)
    return ordered(
        functools.partial(final_kernel, len(groups)),
        after,
        tuple(arrays),
        in_specs=[VSPEC] * len(arrays),
        out_specs=VSPEC,
        out_shape=jax.ShapeDtypeStruct((tok, rows), BF16),
        cost_estimate=cost(rows * tok, 8 * rows * tok),
        name="final",
    )


LINE = ((3, 2, 1, 0, 0), (3, 3, 2, 0, 1), (0, 0, 3, 1, 2), (0, 1, 3, 2, 3))


def line_close(one, firsts, head):
    send = lambda array, pairs: lax.ppermute(array, head, pairs)
    seconds = []
    for part, first in enumerate(firsts):
        total = one(1, part, got=(first,))
        seconds.append((send(total, [(0, 1), (1, 2)]), send(total, [(3, 2), (2, 1)])))
    thirds = []
    for part, (right, left) in enumerate(seconds):
        upward = one(2, part, got=(right,))
        downward = one(3, part, got=(left,))
        thirds.append(
            [send(upward, [(0, 1), (1, 2), (2, 3)]), send(downward, [(3, 2), (2, 1), (1, 0)])]
        )
    return thirds


def body(x, q_weight, kv_weight, norm_gain, out_grad):
    seq, head = "seq", "head"
    count, n = lax.axis_size(seq), lax.axis_size(head)
    levels = (count - 1).bit_length()
    place = lax.axis_index(seq)
    bits = jnp.stack([(place >> i) & 1 for i in range(levels)]).astype(jnp.int32)
    same = (place & 1).reshape(1).astype(jnp.int32)
    kv_flat = kv_weight.reshape(2 * q_weight.shape[0], HD)

    line = jnp.array(LINE, jnp.int32)[lax.axis_index(head) % 4]
    kv, state, wkv = kv_project(x, kv_flat)
    states, q = doubling(state, seq, levels, lambda got: q_project(x, q_weight, after=(got,)))
    o = intra(q, kv, after=states[1:2])
    dq, do, own = grad_step(bits, q, o, kv, norm_gain, out_grad, states)
    laters, inner = doubling(
        own, seq, levels, lambda got: inner_step(q, do, kv, after=(got,))
    )
    grads = outer_step(1 - bits, inner, kv, dq, laters)

    filling = []
    if n == 4:
        one = functools.partial(
            partial, parts=PARTS, ids=line, q_weight=q_weight, wkv=wkv, grads=grads, n=n
        )
        filling = [one(0, part, got=()) for part in range(PARTS)]
        firsts = [lax.ppermute(array, head, [(0, 1), (3, 2)]) for array in filling]
    got = flip(weight_send(1 - same, x, grads, seq), seq, 0)
    high, low = weight_keep(x, grads, got, seq, after=filling)
    for bit in range(levels - 1, 0, -1):
        got = flip(high, seq, bit)
        if bit > 1:
            high, low = fold(low, got)
    parts = [low, got]
    q_grad, kv_grad = weight_last(parts)
    if n == 4:
        own_terms = [one(4, part, got=()) for part in range(PARTS)]
        thirds = line_close(one, firsts, head)
        groups = [[mine] + third for mine, third in zip(own_terms, thirds)]
        input_grad = final(groups, after=(q_grad,))
    else:
        both = jnp.concatenate([q_weight, wkv], axis=1)
        whole = lax.dot_general(
            grads, both, (((0,), (1,)), ((), ())), preferred_element_type=F32
        )
        input_grad = lax.psum_scatter(
            whole.astype(BF16), head, scatter_dimension=1, tiled=True
        )
    return input_grad, q_grad, kv_grad


def solution(mesh):
    return jax.shard_map(
        body,
        mesh=mesh,
        in_specs=(
            P("seq", None),
            P(None, "head"),
            P(None, None, "head"),
            P("head"),
            P("seq", "head"),
        ),
        out_specs=(P("seq", "head"), P("seq", "head"), P("seq", None, "head")),
        check_vma=False,
    )
```

time: 138 us -> 135 us (0.978)
  waiting for transfers between devices: 65.5 us -> 36.8 us
  starting transfers between devices: 11.8 us -> 37 us
  Pallas kernels: 27.9 us -> 41.9 us
  between operations: 14.3 us -> 0.97 us
  matrix products: 5.76 us -> 0 us
  local copies, waits for them, and re-layouts: 12 us -> 17.7 us
    ppermute x12 -> x9, waiting for transfers between devices: 40.6 us -> 8.3 us  [flip(): return lax.ppermute(array, axis, [(i, i ^ 1 << bit) for i in range(count)])]
    ppermute x0 -> x10, waiting for transfers between devices: none -> 28.5 us  [the longest x2 15 us: body(): firsts = [lax.ppermute(array, head, [(0, 1), (3, 2)]) for array in filling]]
    ppermute x0 -> x10, starting transfers between devices: none -> 28.3 us  [the longest x8 23.4 us: line_close(): send = lambda array, pairs: lax.ppermute(array, head, pairs)]
    reduce_scatter x1 -> x0, waiting for transfers between devices: 24.8 us -> none  [body(): lax.psum_scatter(partial.astype(BF16), head, scatter_dimension=1, tiled=T...]
    pallas_call x11 -> x25, Pallas kernels: 27.9 us -> 41.9 us  [ordered(): pl.pallas_call(run, grid_spec=pltpu.PrefetchScalarGridSpec(num_scalar_pre...]
    dot_general x2 -> x0, matrix products: 5.76 us -> none  [the longest x1 4.47 us: body(): partial = jnp.dot(dq, q_weight.T, preferred_element_type=F32)]
    unnamed x26 -> x30, local copies, waits for them, and re-layouts: 11.9 us -> 17.1 us
    ppermute x12 -> x9, starting transfers between devices: 11.7 us -> 8.77 us  [flip(): return lax.ppermute(array, axis, [(i, i ^ 1 << bit) for i in range(count)])]
  transfers between devices with their start and end apart: 13 -> 19, of which waited for: 10 -> 13; matrix products, arithmetic and copies ran while one was open for 0% -> 1% of each run, Pallas kernels for 14% -> 17%
where the time goes in v2:
time: 135 us
  Pallas kernels  41.9 us (31%)
  starting transfers between devices  37 us (27%)
  waiting for transfers between devices  36.8 us (27%)
  local copies, waits for them, and re-layouts  17.7 us (13%)
    pallas_call x25, Pallas kernels, ordered(): pl.pallas_call(run, grid_spec=pltpu.PrefetchScalarGridSpec(num_scalar_pre...  41.9 us
    ppermute x8, starting transfers between devices, line_close(): send = lambda array, pairs: lax.ppermute(array, head, pairs)  23.4 us
    unnamed x30, local copies, waits for them, and re-layouts  17.1 us
    ppermute x2, waiting for transfers between devices, body(): firsts = [lax.ppermute(array, head, [(0, 1), (3, 2)]) for array in filling]  15 us
    ppermute x8, waiting for transfers between devices, line_close(): send = lambda array, pairs: lax.ppermute(array, head, pairs)  13.5 us
    ppermute x9, starting transfers between devices, flip(): return lax.ppermute(array, axis, [(i, i ^ 1 << bit) for i in range(count)])  8.77 us
    ppermute x9, waiting for transfers between devices, flip(): return lax.ppermute(array, axis, [(i, i ^ 1 << bit) for i in range(count)])  8.3 us
    ppermute x2, starting transfers between devices, body(): firsts = [lax.ppermute(array, head, [(0, 1), (3, 2)]) for array in filling]  4.81 us
  transfers between devices with their start and end apart: 19, of which 13 were waited for; matrix products, arithmetic and copies ran while one was open for 1% of the time, Pallas kernels for 17%

profile of v2, /device:TPU:0, one launch (start us, length us, event | category | flops | bytes accessed | tf_op | source)
XLA Modules:
  0.0 134.5 jit_solution(7741301890136657659)
XLA Ops:
  0.6 2.2 %copy-done.3 = bf16[512,4096]{1,0:T(8,128)(2,1)S(1)} copy-done((bf16[512,4096]{1,0:T(8,128)(2,1)S(1)}, bf16[512,4096]{1,0:T(8,128)(2,1)}, u32[]{:S(2)}) %copy-start.3) | copy-done | bytes 4194328
  2.8 1.6 %copy-done.9 = bf16[4096,2,128]{2,1,0:T(2,128)(2,1)S(1)} copy-done((bf16[4096,2,128]{2,1,0:T(2,128)(2,1)S(1)}, bf16[4096,2,128]{2,1,0:T(2,128)(2,1)}, u32[]{:S(2)}) %copy-start.9) | copy-done | bytes 2097176
  4.4 3.9 %kv_project.1 = (bf16[512,256]{1,0:T(8,128)(2,1)S(1)}, bf16[128,128]{1,0:T(8,128)(2,1)S(1)}, bf16[4096,256]{1,0:T(8,128)(2,1)S(1)}) custom-call(bf16[512,4096]{1,0:T(8,128)(2,1)S(1)} %copy-done.3, bf16[8192,128]{1,0:T(8,128)(2,1)S(1)} %bitcast.13), custom_call_target="tpu_custom_call" | custom-call | flops 16777216 | bytes 131072 | tf_op jit(solution)/shard_map/kv_project/pallas_call | solution.py:49
  9.7 2.9 %collective-permute-start.1 = (bf16[128,128]{1,0:T(8,128)(2,1)S(1)}, bf16[128,128]{1,0:T(8,128)(2,1)S(1)}, u32[]{:S(2)}, u32[]{:S(2)}) collective-permute-start(bf16[128,128]{1,0:T(8,128)(2,1)S(1)} %merge.4.refs_0_), channel_id=1, source_target_pairs={{0,8},{4,12},{8,0},{12,4},{16,24},{20,28},{24,16},{28,20},{1,9},{5... | collective-permute-start | bytes 98312 | tf_op jit(solution)/shard_map/ppermute | solution.py:434
  12.6 2.2 %copy-done = bf16[4096,512]{1,0:T(8,128)(2,1)S(1)} copy-done((bf16[4096,512]{1,0:T(8,128)(2,1)S(1)}, bf16[4096,512]{1,0:T(8,128)(2,1)}, u32[]{:S(2)}) %copy-start) | copy-done | bytes 4194328
  14.8 2.2 %copy-done.4 = bf16[512,4096]{1,0:T(8,128)(2,1)S(1)} copy-done((bf16[512,4096]{1,0:T(8,128)(2,1)S(1)}, bf16[512,4096]{1,0:T(8,128)(2,1)}, u32[]{:S(2)}) %copy-start.4) | copy-done | bytes 4194328
  17.0 3.5 %q_project.1.refs_0_.refs_2_.refs_1_ = bf16[512,512]{1,0:T(8,128)(2,1)S(1)} custom-call(bf16[512,4096]{1,0:T(8,128)(2,1)S(1)} %copy-done.4, bf16[4096,512]{1,0:T(8,128)(2,1)S(1)} %copy-done, bf16[128,128]{1,0:T(8,128)(2,1)S(1)} %collective-permute-done.refs_2_.refs_1_.refs_6_), custom_call_target="tpu_custom_call" | custom-call | flops 33554432 | bytes 131072 | tf_op jit(solution)/shard_map/q_project/pallas_call | solution.py:49
  20.6 1.6 %collective-permute-start.2 = (bf16[128,128]{1,0:T(8,128)(2,1)S(1)}, bf16[128,128]{1,0:T(8,128)(2,1)S(1)}, u32[]{:S(2)}, u32[]{:S(2)}) collective-permute-start(bf16[128,128]{1,0:T(8,128)(2,1)S(1)} %merge.5), channel_id=1, source_target_pairs={{0,16},{4,20},{8,24},{12,28},{16,0},{20,4},{24,8},{28,12},{1,17},{... | collective-permute-start | bytes 98312 | tf_op jit(solution)/shard_map/ppermute | solution.py:434
  22.2 1.4 %intra.1.refs_2_ = f32[512,512]{1,0:T(8,128)S(1)} custom-call(bf16[512,512]{1,0:T(8,128)(2,1)S(1)} %q_project.1.refs_0_.refs_2_.refs_1_, bf16[512,256]{1,0:T(8,128)(2,1)S(1)} %get-tuple-element.17.refs_1_.refs_3_.refs_2_, bf16[128,128]{1,0:T(8,128)(2,1)S(1)} %collective-permute-done.1.refs_2_.refs_1_.refs_7_), custom_call_target="tpu_custom_call" | custom-call | flops 8388608 | bytes 24576 | tf_op jit(solution)/shard_map/intra/pallas_call | solution.py:49
  24.6 3.9 %grad_step.1 = (bf16[512,512]{1,0:T(8,128)(2,1)S(1)}, bf16[512,512]{1,0:T(8,128)(2,1)S(1)}, bf16[128,128]{1,0:T(8,128)(2,1)S(1)}) custom-call(s32[3]{0:T(128)S(1)} %get-tuple-element.28.refs_0_, bf16[512,512]{1,0:T(8,128)(2,1)S(1)} %q_project.1.refs_0_.refs_2_.refs_1_, f32[512,512]{1,0:T(8,128)S(1)} %intra.1.refs_2_, ...), custom_call_target="tpu_custom_call" | custom-call | flops 16777216 | bytes 49152 | tf_op jit(solution)/shard_map/grad_step/pallas_call | solution.py:49
  30.6 2.2 %inner_step.1.refs_2_.refs_1_ = f32[512,256]{1,0:T(8,128)S(1)} custom-call(bf16[512,512]{1,0:T(8,128)(2,1)S(1)} %q_project.1.refs_0_.refs_2_.refs_1_, bf16[512,512]{1,0:T(8,128)(2,1)S(1)} %get-tuple-element.18.refs_1_, bf16[512,256]{1,0:T(8,128)(2,1)S(1)} %get-tuple-element.17.refs_1_.refs_3_.refs_2_, ...), custom_call_target="tpu_custom_call" | custom-call | flops 16777216 | bytes 32768 | tf_op jit(solution)/shard_map/inner_step/pallas_call | solution.py:49
  32.8 1.6 %collective-permute-done.4.refs_1_.refs_5_ = bf16[128,128]{1,0:T(8,128)(2,1)S(1)} collective-permute-done((bf16[128,128]{1,0:T(8,128)(2,1)S(1)}, bf16[128,128]{1,0:T(8,128)(2,1)S(1)}, u32[]{:S(2)}, u32[]{:S(2)}) %collective-permute-start.4) | collective-permute-done | bytes 32800 | tf_op jit(solution)/shard_map/ppermute | solution.py:434
  34.5 1.6 %collective-permute-start.5 = (bf16[128,128]{1,0:T(8,128)(2,1)S(1)}, bf16[128,128]{1,0:T(8,128)(2,1)S(1)}, u32[]{:S(2)}, u32[]{:S(2)}) collective-permute-start(bf16[128,128]{1,0:T(8,128)(2,1)S(1)} %merge.7), channel_id=1, source_target_pairs={{0,16},{4,20},{8,24},{12,28},{16,0},{20,4},{24,8},{28,12},{1,17},{... | collective-permute-start | bytes 98312 | tf_op jit(solution)/shard_map/ppermute | solution.py:434
  36.1 2.4 %collective-permute-done.5.refs_6_ = bf16[128,128]{1,0:T(8,128)(2,1)S(1)} collective-permute-done((bf16[128,128]{1,0:T(8,128)(2,1)S(1)}, bf16[128,128]{1,0:T(8,128)(2,1)S(1)}, u32[]{:S(2)}, u32[]{:S(2)}) %collective-permute-start.5) | collective-permute-done | bytes 32800 | tf_op jit(solution)/shard_map/ppermute | solution.py:434
  41.4 2.2 %copy-done.5 = bf16[512,4096]{1,0:T(8,128)(2,1)S(1)} copy-done((bf16[512,4096]{1,0:T(8,128)(2,1)S(1)}, bf16[512,4096]{1,0:T(8,128)(2,1)}, u32[]{:S(2)}) %copy-start.5) | copy-done | bytes 4194328
  43.5 3.7 %weight_send.1 = bf16[4,768,512]{2,1,0:T(8,128)(2,1)} custom-call(s32[1]{0:T(128)} %bitcast.10.refs_0_, bf16[512,4096]{1,0:T(8,128)(2,1)S(1)} %copy-done.5, bf16[768,512]{1,0:T(8,128)(2,1)S(1)} %outer_step.1.refs_3_.refs_2_), custom_call_target="tpu_custom_call" | custom-call | flops 25165824 | bytes 81920 | tf_op jit(solution)/shard_map/weight_send/pallas_call | solution.py:49
  48.0 2.2 %copy-done.1 = bf16[4096,512]{1,0:T(8,128)(2,1)S(1)} copy-done((bf16[4096,512]{1,0:T(8,128)(2,1)S(1)}, bf16[4096,512]{1,0:T(8,128)(2,1)}, u32[]{:S(2)}) %copy-start.1) | copy-done | bytes 4194328
  53.7 5.3 %weight_keep.1 = (bf16[2,768,512]{2,1,0:T(8,128)(2,1)S(1)}, bf16[2,768,512]{2,1,0:T(8,128)(2,1)S(1)}) custom-call(s32[4]{0:T(128)S(1)} %pad_add_fusion.1.refs_0_, bf16[512,4096]{1,0:T(8,128)(2,1)S(1)} %copy-done.6, bf16[768,512]{1,0:T(8,128)(2,1)S(1)} %outer_step.1.refs_3_.refs_2_, bf16[4,768,512]{2,1,0:T(8,128)(2,1)} %collective-permute-done.16.refs_3_, ...), custom_call_target="tpu_custom_call" | custom-call | flops 25165824 | bytes 131072 | tf_op jit(solution)/shard_map/weight_keep/pallas_call | solution.py:49
  59.0 1.6 %collective-permute-start.17 = (bf16[2,768,512]{2,1,0:T(8,128)(2,1)S(1)}, bf16[2,768,512]{2,1,0:T(8,128)(2,1)S(1)}, u32[]{:S(2)}, u32[]{:S(2)}) collective-permute-start(bf16[2,768,512]{2,1,0:T(8,128)(2,1)S(1)} %get-tuple-element.22), channel_id=1, source_target_pairs={{0,16},{4,20},{8,24},{12,28},{16,0},{20,4},{24,8},{28,12},{1,17},{... | collective-permute-start | bytes 4718600 | tf_op jit(solution)/shard_map/ppermute | solution.py:434
  60.6 3.5 %collective-permute-start.11 = (bf16[1024,256]{1,0:T(8,128)(2,1)S(1)}, bf16[1024,256]{1,0:T(8,128)(2,1)S(1)}, u32[]{:S(2)}, u32[]{:S(2)}) collective-permute-start(bf16[1024,256]{1,0:T(8,128)(2,1)S(1)} %partial.16.refs_5_), channel_id=1, source_target_pairs={{0,1},{3,2},{4,5},{7,6},{8,9},{11,10},{12,13},{15,14},{16,17},{19,... | collective-permute-start | bytes 1572872 | tf_op jit(solution)/shard_map/ppermute | solution.py:573
  65.4 10.9 %collective-permute-done.11.refs_4_ = bf16[1024,256]{1,0:T(8,128)(2,1)S(1)} collective-permute-done((bf16[1024,256]{1,0:T(8,128)(2,1)S(1)}, bf16[1024,256]{1,0:T(8,128)(2,1)S(1)}, u32[]{:S(2)}, u32[]{:S(2)}) %collective-permute-start.11) | collective-permute-done | bytes 524320 | tf_op jit(solution)/shard_map/ppermute | solution.py:573
  78.4 5.0 %collective-permute-start.12 = (bf16[1024,256]{1,0:T(8,128)(2,1)S(1)}, bf16[1024,256]{1,0:T(8,128)(2,1)S(1)}, u32[]{:S(2)}, u32[]{:S(2)}) collective-permute-start(bf16[1024,256]{1,0:T(8,128)(2,1)S(1)} %partial.17), channel_id=1, source_target_pairs={{0,1},{1,2},{4,5},{5,6},{8,9},{9,10},{12,13},{13,14},{16,17},{17,1... | collective-permute-start | bytes 1572872 | tf_op jit(solution)/shard_map/ppermute | solution.py:533
  83.4 4.1 %collective-permute-done.6.refs_4_ = bf16[1024,256]{1,0:T(8,128)(2,1)S(1)} collective-permute-done((bf16[1024,256]{1,0:T(8,128)(2,1)S(1)}, bf16[1024,256]{1,0:T(8,128)(2,1)S(1)}, u32[]{:S(2)}, u32[]{:S(2)}) %collective-permute-start.6) | collective-permute-done | bytes 524320 | tf_op jit(solution)/shard_map/ppermute | solution.py:573
  89.7 5.2 %collective-permute-start.7 = (bf16[1024,256]{1,0:T(8,128)(2,1)S(1)}, bf16[1024,256]{1,0:T(8,128)(2,1)S(1)}, u32[]{:S(2)}, u32[]{:S(2)}) collective-permute-start(bf16[1024,256]{1,0:T(8,128)(2,1)S(1)} %partial.12), channel_id=1, source_target_pairs={{0,1},{1,2},{4,5},{5,6},{8,9},{9,10},{12,13},{13,14},{16,17},{17,1... | collective-permute-start | bytes 1572872 | tf_op jit(solution)/shard_map/ppermute | solution.py:533
  99.4 1.4 %partial.18 = bf16[1024,256]{1,0:T(8,128)(2,1)S(1)} custom-call(s32[5]{0:T(128)S(1)} %dynamic-slice_bitcast_fusion.refs_0_, bf16[4096,512]{1,0:T(8,128)(2,1)S(1)} %copy-done.2, bf16[4096,256]{1,0:T(8,128)(2,1)S(1)} %get-tuple-element.15.refs_2_, bf16[768,512]{1,0:T(8,128)(2,1)S(1)} %outer_step.1.refs_3_.refs_2_, ...), custom_call_target="tpu_custom_call" | custom-call | flops 6291456 | bytes 40960 | tf_op jit(solution)/shard_map/partial/pallas_call | solution.py:49
  100.8 4.6 %collective-permute-start.13 = (bf16[1024,256]{1,0:T(8,128)(2,1)S(1)}, bf16[1024,256]{1,0:T(8,128)(2,1)S(1)}, u32[]{:S(2)}, u32[]{:S(2)}) collective-permute-start(bf16[1024,256]{1,0:T(8,128)(2,1)S(1)} %partial.18), channel_id=1, source_target_pairs={{0,1},{1,2},{2,3},{4,5},{5,6},{6,7},{8,9},{9,10},{10,11},{12,13},{... | collective-permute-start | bytes 1572872 | tf_op jit(solution)/shard_map/ppermute | solution.py:533
  108.0 2.0 %collective-permute-done.7.refs_4_ = bf16[1024,256]{1,0:T(8,128)(2,1)S(1)} collective-permute-done((bf16[1024,256]{1,0:T(8,128)(2,1)S(1)}, bf16[1024,256]{1,0:T(8,128)(2,1)S(1)}, u32[]{:S(2)}, u32[]{:S(2)}) %collective-permute-start.7) | collective-permute-done | bytes 524320 | tf_op jit(solution)/shard_map/ppermute | solution.py:533
  111.4 4.7 %collective-permute-start.8 = (bf16[1024,256]{1,0:T(8,128)(2,1)S(1)}, bf16[1024,256]{1,0:T(8,128)(2,1)S(1)}, u32[]{:S(2)}, u32[]{:S(2)}) collective-permute-start(bf16[1024,256]{1,0:T(8,128)(2,1)S(1)} %partial.13), channel_id=1, source_target_pairs={{0,1},{1,2},{2,3},{4,5},{5,6},{6,7},{8,9},{9,10},{10,11},{12,13},{... | collective-permute-start | bytes 1572872 | tf_op jit(solution)/shard_map/ppermute | solution.py:533
  118.9 1.5 %weight_last.1 = (f32[512,512]{1,0:T(8,128)}, f32[1024,128]{1,0:T(8,128)}) custom-call(bf16[1,768,512]{2,1,0:T(8,128)(2,1)S(1)} %get-tuple-element.23.refs_0_, bf16[1,768,512]{2,1,0:T(8,128)(2,1)S(1)} %collective-permute-done.18.refs_1_), custom_call_target="tpu_custom_call" | custom-call | flops 4096 | bytes 32768 | tf_op jit(solution)/shard_map/weight_last/pallas_call | solution.py:49
  121.3 3.2 %collective-permute-done.10.refs_2_ = bf16[1024,256]{1,0:T(8,128)(2,1)S(1)} collective-permute-done((bf16[1024,256]{1,0:T(8,128)(2,1)S(1)}, bf16[1024,256]{1,0:T(8,128)(2,1)S(1)}, u32[]{:S(2)}, u32[]{:S(2)}) %collective-permute-start.10) | collective-permute-done | bytes 524320 | tf_op jit(solution)/shard_map/ppermute | solution.py:533
  124.5 7.3 %collective-permute-done.8.refs_1_ = bf16[1024,256]{1,0:T(8,128)(2,1)S(1)} collective-permute-done((bf16[1024,256]{1,0:T(8,128)(2,1)S(1)}, bf16[1024,256]{1,0:T(8,128)(2,1)S(1)}, u32[]{:S(2)}, u32[]{:S(2)}) %collective-permute-start.8) | collective-permute-done | bytes 524320 | tf_op jit(solution)/shard_map/ppermute | solution.py:533
  133.0 1.5 %final.1 = bf16[512,1024]{1,0:T(8,128)(2,1)} custom-call(bf16[1024,256]{1,0:T(8,128)(2,1)S(1)} %partial.10.refs_0_, bf16[1024,256]{1,0:T(8,128)(2,1)S(1)} %collective-permute-done.8.refs_1_, bf16[1024,256]{1,0:T(8,128)(2,1)S(1)} %collective-permute-done.10.refs_2_, bf16[1024,256]{1,0:T(8,128)(2,1)S(1)} %partial.15.refs_3_, ...), custom_call_target="tpu_custom_call" | custom-call | flops 8192 | bytes 65536 | tf_op jit(solution)/shard_map/final/pallas_call | solution.py:49
  (64 shorter events, 30.6 us)
Async XLA Ops:
  0.6 2.2 %copy-start.3 = (bf16[512,4096]{1,0:T(8,128)(2,1)S(1)}, bf16[512,4096]{1,0:T(8,128)(2,1)}, u32[]{:S(2)}) copy-start(bf16[512,4096]{1,0:T(8,128)(2,1)} %refs_1_.25) | copy-start | bytes 12582916
  2.8 1.6 %copy-start.9 = (bf16[4096,2,128]{2,1,0:T(2,128)(2,1)S(1)}, bf16[4096,2,128]{2,1,0:T(2,128)(2,1)}, u32[]{:S(2)}) copy-start(bf16[4096,2,128]{2,1,0:T(2,128)(2,1)} %param.8) | copy-start | bytes 6291460
  8.3 22.3 %copy-start.7 = (bf16[512,256]{1,0:T(8,128)(2,1)}, bf16[512,256]{1,0:T(8,128)(2,1)S(1)}, u32[]{:S(2)}) copy-start(bf16[512,256]{1,0:T(8,128)(2,1)S(1)} %get-tuple-element.17.refs_1_.refs_3_.refs_2_) | copy-start | bytes 786436
  8.3 1.4 %collective-permute-start = (bf16[128,128]{1,0:T(8,128)(2,1)S(1)}, bf16[128,128]{1,0:T(8,128)(2,1)S(1)}, u32[]{:S(2)}, u32[]{:S(2)}) collective-permute-start(bf16[128,128]{1,0:T(8,128)(2,1)S(1)} %get-tuple-element.16.refs_0_), channel_id=1, source_target_pairs={{0,4},{4,0},{8,12},{12,8},{16,20},{20,16},{24,28},{28,24},{1,5},{5... | collective-permute-start | bytes 98312 | tf_op jit(solution)/shard_map/ppermute | solution.py:434
  9.7 10.8 %collective-permute-start.1 = (bf16[128,128]{1,0:T(8,128)(2,1)S(1)}, bf16[128,128]{1,0:T(8,128)(2,1)S(1)}, u32[]{:S(2)}, u32[]{:S(2)}) collective-permute-start(bf16[128,128]{1,0:T(8,128)(2,1)S(1)} %merge.4.refs_0_), channel_id=1, source_target_pairs={{0,8},{4,12},{8,0},{12,4},{16,24},{20,28},{24,16},{28,20},{1,9},{5... | collective-permute-start | bytes 98312 | tf_op jit(solution)/shard_map/ppermute | solution.py:434
  12.6 2.2 %copy-start = (bf16[4096,512]{1,0:T(8,128)(2,1)S(1)}, bf16[4096,512]{1,0:T(8,128)(2,1)}, u32[]{:S(2)}) copy-start(bf16[4096,512]{1,0:T(8,128)(2,1)} %refs_1_.23) | copy-start | bytes 12582916
  14.8 2.2 %copy-start.4 = (bf16[512,4096]{1,0:T(8,128)(2,1)S(1)}, bf16[512,4096]{1,0:T(8,128)(2,1)}, u32[]{:S(2)}) copy-start(bf16[512,4096]{1,0:T(8,128)(2,1)} %refs_1_.25) | copy-start | bytes 12582916
  20.5 4.0 %copy-start.13 = (bf16[512,512]{1,0:T(8,128)(2,1)S(1)}, bf16[512,512]{1,0:T(8,128)(2,1)}, u32[]{:S(2)}) copy-start(bf16[512,512]{1,0:T(8,128)(2,1)} %refs_5_.1) | copy-start | bytes 1572868
  20.5 4.0 %copy-start.14 = (f32[512]{0:T(512)S(1)}, f32[512]{0:T(512)}, u32[]{:S(2)}) copy-start(f32[512]{0:T(512)} %param.9) | copy-start | bytes 6148
  20.6 4.0 %collective-permute-start.2 = (bf16[128,128]{1,0:T(8,128)(2,1)S(1)}, bf16[128,128]{1,0:T(8,128)(2,1)S(1)}, u32[]{:S(2)}, u32[]{:S(2)}) collective-permute-start(bf16[128,128]{1,0:T(8,128)(2,1)S(1)} %merge.5), channel_id=1, source_target_pairs={{0,16},{4,20},{8,24},{12,28},{16,0},{20,4},{24,8},{28,12},{1,17},{... | collective-permute-start | bytes 98312 | tf_op jit(solution)/shard_map/ppermute | solution.py:434
  29.3 1.2 collective-permute-start.3
  30.5 4.0 %collective-permute-start.4 = (bf16[128,128]{1,0:T(8,128)(2,1)S(1)}, bf16[128,128]{1,0:T(8,128)(2,1)S(1)}, u32[]{:S(2)}, u32[]{:S(2)}) collective-permute-start(bf16[128,128]{1,0:T(8,128)(2,1)S(1)} %merge.6.refs_0_), channel_id=1, source_target_pairs={{0,8},{4,12},{8,0},{12,4},{16,24},{20,28},{24,16},{28,20},{1,9},{5... | collective-permute-start | bytes 98312 | tf_op jit(solution)/shard_map/ppermute | solution.py:434
  34.5 4.0 %collective-permute-start.5 = (bf16[128,128]{1,0:T(8,128)(2,1)S(1)}, bf16[128,128]{1,0:T(8,128)(2,1)S(1)}, u32[]{:S(2)}, u32[]{:S(2)}) collective-permute-start(bf16[128,128]{1,0:T(8,128)(2,1)S(1)} %merge.7), channel_id=1, source_target_pairs={{0,16},{4,20},{8,24},{12,28},{16,0},{20,4},{24,8},{28,12},{1,17},{... | collective-permute-start | bytes 98312 | tf_op jit(solution)/shard_map/ppermute | solution.py:434
  39.4 1.0 copy-start.12
  41.4 2.2 %copy-start.5 = (bf16[512,4096]{1,0:T(8,128)(2,1)S(1)}, bf16[512,4096]{1,0:T(8,128)(2,1)}, u32[]{:S(2)}) copy-start(bf16[512,4096]{1,0:T(8,128)(2,1)} %refs_1_.25) | copy-start | bytes 12582916
  47.2 6.0 %collective-permute-start.16 = (bf16[4,768,512]{2,1,0:T(8,128)(2,1)}, bf16[4,768,512]{2,1,0:T(8,128)(2,1)}, u32[]{:S(2)}, u32[]{:S(2)}) collective-permute-start(bf16[4,768,512]{2,1,0:T(8,128)(2,1)} %weight_send.1), channel_id=1, source_target_pairs={{0,4},{4,0},{8,12},{12,8},{16,20},{20,16},{24,28},{28,24},{1,5},{5... | collective-permute-start | bytes 9437192 | tf_op jit(solution)/shard_map/ppermute | solution.py:434
  48.0 2.2 %copy-start.1 = (bf16[4096,512]{1,0:T(8,128)(2,1)S(1)}, bf16[4096,512]{1,0:T(8,128)(2,1)}, u32[]{:S(2)}) copy-start(bf16[4096,512]{1,0:T(8,128)(2,1)} %refs_1_.23) | copy-start | bytes 12582916
  51.5 2.2 %copy-start.6 = (bf16[512,4096]{1,0:T(8,128)(2,1)S(1)}, bf16[512,4096]{1,0:T(8,128)(2,1)}, u32[]{:S(2)}) copy-start(bf16[512,4096]{1,0:T(8,128)(2,1)} %refs_1_.25) | copy-start | bytes 12582916
  53.7 22.6 %copy-start.2 = (bf16[4096,512]{1,0:T(8,128)(2,1)S(1)}, bf16[4096,512]{1,0:T(8,128)(2,1)}, u32[]{:S(2)}) copy-start(bf16[4096,512]{1,0:T(8,128)(2,1)} %refs_1_.23) | copy-start | bytes 12582916
  59.0 36.9 %collective-permute-start.17 = (bf16[2,768,512]{2,1,0:T(8,128)(2,1)S(1)}, bf16[2,768,512]{2,1,0:T(8,128)(2,1)S(1)}, u32[]{:S(2)}, u32[]{:S(2)}) collective-permute-start(bf16[2,768,512]{2,1,0:T(8,128)(2,1)S(1)} %get-tuple-element.22), channel_id=1, source_target_pairs={{0,16},{4,20},{8,24},{12,28},{16,0},{20,4},{24,8},{28,12},{1,17},{... | collective-permute-start | bytes 4718600 | tf_op jit(solution)/shard_map/ppermute | solution.py:434
  60.6 15.7 %collective-permute-start.11 = (bf16[1024,256]{1,0:T(8,128)(2,1)S(1)}, bf16[1024,256]{1,0:T(8,128)(2,1)S(1)}, u32[]{:S(2)}, u32[]{:S(2)}) collective-permute-start(bf16[1024,256]{1,0:T(8,128)(2,1)S(1)} %partial.16.refs_5_), channel_id=1, source_target_pairs={{0,1},{3,2},{4,5},{7,6},{8,9},{11,10},{12,13},{15,14},{16,17},{19,... | collective-permute-start | bytes 1572872 | tf_op jit(solution)/shard_map/ppermute | solution.py:573
  64.1 23.5 %collective-permute-start.6 = (bf16[1024,256]{1,0:T(8,128)(2,1)S(1)}, bf16[1024,256]{1,0:T(8,128)(2,1)S(1)}, u32[]{:S(2)}, u32[]{:S(2)}) collective-permute-start(bf16[1024,256]{1,0:T(8,128)(2,1)S(1)} %partial.11.refs_4_), channel_id=1, source_target_pairs={{0,1},{3,2},{4,5},{7,6},{8,9},{11,10},{12,13},{15,14},{16,17},{19,... | collective-permute-start | bytes 1572872 | tf_op jit(solution)/shard_map/ppermute | solution.py:573
  77.7 19.0 %collective-permute-start.14 = (bf16[1024,256]{1,0:T(8,128)(2,1)S(1)}, bf16[1024,256]{1,0:T(8,128)(2,1)S(1)}, u32[]{:S(2)}, u32[]{:S(2)}) collective-permute-start(bf16[1024,256]{1,0:T(8,128)(2,1)S(1)} %partial.17), channel_id=1, source_target_pairs={{3,2},{2,1},{7,6},{6,5},{11,10},{10,9},{15,14},{14,13},{19,18},{18... | collective-permute-start | bytes 1572872 | tf_op jit(solution)/shard_map/ppermute | solution.py:533
  78.4 21.0 %collective-permute-start.12 = (bf16[1024,256]{1,0:T(8,128)(2,1)S(1)}, bf16[1024,256]{1,0:T(8,128)(2,1)S(1)}, u32[]{:S(2)}, u32[]{:S(2)}) collective-permute-start(bf16[1024,256]{1,0:T(8,128)(2,1)S(1)} %partial.17), channel_id=1, source_target_pairs={{0,1},{1,2},{4,5},{5,6},{8,9},{9,10},{12,13},{13,14},{16,17},{17,1... | collective-permute-start | bytes 1572872 | tf_op jit(solution)/shard_map/ppermute | solution.py:533
  89.0 16.4 %collective-permute-start.9 = (bf16[1024,256]{1,0:T(8,128)(2,1)S(1)}, bf16[1024,256]{1,0:T(8,128)(2,1)S(1)}, u32[]{:S(2)}, u32[]{:S(2)}) collective-permute-start(bf16[1024,256]{1,0:T(8,128)(2,1)S(1)} %partial.12), channel_id=1, source_target_pairs={{3,2},{2,1},{7,6},{6,5},{11,10},{10,9},{15,14},{14,13},{19,18},{18... | collective-permute-start | bytes 1572872 | tf_op jit(solution)/shard_map/ppermute | solution.py:533
  89.7 20.4 %collective-permute-start.7 = (bf16[1024,256]{1,0:T(8,128)(2,1)S(1)}, bf16[1024,256]{1,0:T(8,128)(2,1)S(1)}, u32[]{:S(2)}, u32[]{:S(2)}) collective-permute-start(bf16[1024,256]{1,0:T(8,128)(2,1)S(1)} %partial.12), channel_id=1, source_target_pairs={{0,1},{1,2},{4,5},{5,6},{8,9},{9,10},{12,13},{13,14},{16,17},{17,1... | collective-permute-start | bytes 1572872 | tf_op jit(solution)/shard_map/ppermute | solution.py:533
  96.3 22.6 %collective-permute-start.18 = (bf16[1,768,512]{2,1,0:T(8,128)(2,1)S(1)}, bf16[1,768,512]{2,1,0:T(8,128)(2,1)S(1)}, u32[]{:S(2)}, u32[]{:S(2)}) collective-permute-start(bf16[1,768,512]{2,1,0:T(8,128)(2,1)S(1)} %get-tuple-element.24), channel_id=1, source_target_pairs={{0,8},{4,12},{8,0},{12,4},{16,24},{20,28},{24,16},{28,20},{1,9},{5... | collective-permute-start | bytes 2359304 | tf_op jit(solution)/shard_map/ppermute | solution.py:434
  98.1 22.3 %collective-permute-start.15 = (bf16[1024,256]{1,0:T(8,128)(2,1)S(1)}, bf16[1024,256]{1,0:T(8,128)(2,1)S(1)}, u32[]{:S(2)}, u32[]{:S(2)}) collective-permute-start(bf16[1024,256]{1,0:T(8,128)(2,1)S(1)} %partial.19), channel_id=1, source_target_pairs={{3,2},{2,1},{1,0},{7,6},{6,5},{5,4},{11,10},{10,9},{9,8},{15,14},{... | collective-permute-start | bytes 1572872 | tf_op jit(solution)/shard_map/ppermute | solution.py:533
  100.8 20.5 %collective-permute-start.13 = (bf16[1024,256]{1,0:T(8,128)(2,1)S(1)}, bf16[1024,256]{1,0:T(8,128)(2,1)S(1)}, u32[]{:S(2)}, u32[]{:S(2)}) collective-permute-start(bf16[1024,256]{1,0:T(8,128)(2,1)S(1)} %partial.18), channel_id=1, source_target_pairs={{0,1},{1,2},{2,3},{4,5},{5,6},{6,7},{8,9},{9,10},{10,11},{12,13},{... | collective-permute-start | bytes 1572872 | tf_op jit(solution)/shard_map/ppermute | solution.py:533
  106.7 17.8 %collective-permute-start.10 = (bf16[1024,256]{1,0:T(8,128)(2,1)S(1)}, bf16[1024,256]{1,0:T(8,128)(2,1)S(1)}, u32[]{:S(2)}, u32[]{:S(2)}) collective-permute-start(bf16[1024,256]{1,0:T(8,128)(2,1)S(1)} %partial.14), channel_id=1, source_target_pairs={{3,2},{2,1},{1,0},{7,6},{6,5},{5,4},{11,10},{10,9},{9,8},{15,14},{... | collective-permute-start | bytes 1572872 | tf_op jit(solution)/shard_map/ppermute | solution.py:533
  111.4 20.4 %collective-permute-start.8 = (bf16[1024,256]{1,0:T(8,128)(2,1)S(1)}, bf16[1024,256]{1,0:T(8,128)(2,1)S(1)}, u32[]{:S(2)}, u32[]{:S(2)}) collective-permute-start(bf16[1024,256]{1,0:T(8,128)(2,1)S(1)} %partial.13), channel_id=1, source_target_pairs={{0,1},{1,2},{2,3},{4,5},{5,6},{6,7},{8,9},{9,10},{10,11},{12,13},{... | collective-permute-start | bytes 1572872 | tf_op jit(solution)/shard_map/ppermute | solution.py:533
  131.8 1.2 copy-start.10
  (2 other events, 1.7 us)

commit v3 on v2

--- a/solution.py
+++ b/solution.py
@@ -125,6 +125,7 @@
         scratch=[pltpu.VMEM((tok, 2 * HD), F32)],
         cost_estimate=cost(4 * tok * d * HD, 2 * (tok * d + 4 * d * HD)),
         name="kv_project",
+        limit=VMEM_MOST,
     )
 
 
@@ -177,6 +178,7 @@
         scratch=[pltpu.VMEM((tok, cols), F32)],
         cost_estimate=cost(2 * tok * d * cols, 2 * (tok * d + d * cols)),
         name="q_project",
+        limit=VMEM_MOST,
     )
 
 
@@ -396,6 +398,7 @@
         out_shape=jax.ShapeDtypeStruct((count, cols, blk), BF16),
         cost_estimate=cost(2 * tok * cols * blk * count, 2 * count * blk * (tok + cols)),
         name="weight_send",
+        limit=VMEM_MOST,
     )
 
 

time: 135 us -> 133 us (0.985)
  local copies, waits for them, and re-layouts: 17.7 us -> 8.37 us
  Pallas kernels: 41.9 us -> 49.5 us
    unnamed x30 -> x32, local copies, waits for them, and re-layouts: 17.1 us -> 7.68 us
    pallas_call x25, Pallas kernels: 41.9 us -> 49.5 us  [ordered(): pl.pallas_call(run, grid_spec=pltpu.PrefetchScalarGridSpec(num_scalar_pre...]
  transfers between devices with their start and end apart: 19 -> 19, of which waited for: 13 -> 12; matrix products, arithmetic and copies ran while one was open for 1% -> 1% of each run, Pallas kernels for 17% -> 19%
where the time goes in v3:
time: 133 us; the launch traced here: 132 us
  Pallas kernels  49.5 us (37%)
  starting transfers between devices  37.3 us (28%)
  waiting for transfers between devices  35.6 us (27%)
  local copies, waits for them, and re-layouts  8.37 us (6%)
    pallas_call x25, Pallas kernels, ordered(): pl.pallas_call(run, grid_spec=pltpu.PrefetchScalarGridSpec(num_scalar_pre...  49.5 us
    ppermute x8, starting transfers between devices, line_close(): send = lambda array, pairs: lax.ppermute(array, head, pairs)  23.4 us
    ppermute x2, waiting for transfers between devices, body(): firsts = [lax.ppermute(array, head, [(0, 1), (3, 2)]) for array in filling]  15 us
    ppermute x8, waiting for transfers between devices, line_close(): send = lambda array, pairs: lax.ppermute(array, head, pairs)  13.1 us
    ppermute x9, starting transfers between devices, flip(): return lax.ppermute(array, axis, [(i, i ^ 1 << bit) for i in range(count)])  9.04 us
    unnamed x32, local copies, waits for them, and re-layouts  7.68 us
    ppermute x9, waiting for transfers between devices, flip(): return lax.ppermute(array, axis, [(i, i ^ 1 << bit) for i in range(count)])  7.45 us
    ppermute x2, starting transfers between devices, body(): firsts = [lax.ppermute(array, head, [(0, 1), (3, 2)]) for array in filling]  4.82 us
  transfers between devices with their start and end apart: 19, of which 12 were waited for; matrix products, arithmetic and copies ran while one was open for 1% of the time, Pallas kernels for 19%

profile of v3, /device:TPU:0, one launch (start us, length us, event | category | flops | bytes accessed | tf_op | source)
XLA Modules:
  0.0 131.9 jit_solution(1784986330094982305)
XLA Ops:
  0.6 6.7 %kv_project.1 = (bf16[512,256]{1,0:T(8,128)(2,1)}, bf16[128,128]{1,0:T(8,128)(2,1)}, bf16[4096,256]{1,0:T(8,128)(2,1)}) custom-call(bf16[512,4096]{1,0:T(8,128)(2,1)} %refs_1_.25, bf16[8192,128]{1,0:T(8,128)(2,1)} %bitcast.14), custom_call_target="tpu_custom_call" | custom-call | flops 16777216 | bytes 131072 | tf_op jit(solution)/shard_map/kv_project/pallas_call | solution.py:49
  9.7 2.9 %collective-permute-start.1 = (bf16[128,128]{1,0:T(8,128)(2,1)S(1)}, bf16[128,128]{1,0:T(8,128)(2,1)S(1)}, u32[]{:S(2)}, u32[]{:S(2)}) collective-permute-start(bf16[128,128]{1,0:T(8,128)(2,1)S(1)} %merge.4.refs_0_), channel_id=1, source_target_pairs={{0,8},{4,12},{8,0},{12,4},{16,24},{20,28},{24,16},{28,20},{1,9},{5... | collective-permute-start | bytes 98312 | tf_op jit(solution)/shard_map/ppermute | solution.py:437
  12.6 6.5 %q_project.1.refs_0_.refs_2_.refs_1_ = bf16[512,512]{1,0:T(8,128)(2,1)} custom-call(bf16[512,4096]{1,0:T(8,128)(2,1)} %refs_1_.25, bf16[4096,512]{1,0:T(8,128)(2,1)} %refs_1_.23, bf16[128,128]{1,0:T(8,128)(2,1)} %copy-done.12), custom_call_target="tpu_custom_call" | custom-call | flops 33554432 | bytes 131072 | tf_op jit(solution)/shard_map/q_project/pallas_call | solution.py:49
  20.1 1.6 %collective-permute-start.2 = (bf16[128,128]{1,0:T(8,128)(2,1)S(1)}, bf16[128,128]{1,0:T(8,128)(2,1)S(1)}, u32[]{:S(2)}, u32[]{:S(2)}) collective-permute-start(bf16[128,128]{1,0:T(8,128)(2,1)S(1)} %merge.5), channel_id=1, source_target_pairs={{0,16},{4,20},{8,24},{12,28},{16,0},{20,4},{24,8},{28,12},{1,17},{... | collective-permute-start | bytes 98312 | tf_op jit(solution)/shard_map/ppermute | solution.py:437
  22.9 1.4 %intra.1.refs_2_ = f32[512,512]{1,0:T(8,128)S(1)} custom-call(bf16[512,512]{1,0:T(8,128)(2,1)S(1)} %copy-done.7, bf16[512,256]{1,0:T(8,128)(2,1)S(1)} %copy-done.9, bf16[128,128]{1,0:T(8,128)(2,1)S(1)} %collective-permute-done.1.refs_2_.refs_1_.refs_7_), custom_call_target="tpu_custom_call" | custom-call | flops 8388608 | bytes 24576 | tf_op jit(solution)/shard_map/intra/pallas_call | solution.py:49
  24.3 3.9 %grad_step.1 = (bf16[512,512]{1,0:T(8,128)(2,1)S(1)}, bf16[512,512]{1,0:T(8,128)(2,1)S(1)}, bf16[128,128]{1,0:T(8,128)(2,1)S(1)}) custom-call(s32[3]{0:T(128)S(1)} %get-tuple-element.28.refs_0_, bf16[512,512]{1,0:T(8,128)(2,1)S(1)} %copy-done.8, f32[512,512]{1,0:T(8,128)S(1)} %intra.1.refs_2_, bf16[512,256]{1,0:T(8,128)(2,1)S(1)} %copy-done.9, ...), custom_call_target="tpu_custom_call" | custom-call | flops 16777216 | bytes 49152 | tf_op jit(solution)/shard_map/grad_step/pallas_call | solution.py:49
  30.1 2.3 %inner_step.1.refs_2_.refs_1_ = f32[512,256]{1,0:T(8,128)S(1)} custom-call(bf16[512,512]{1,0:T(8,128)(2,1)S(1)} %copy-done.8, bf16[512,512]{1,0:T(8,128)(2,1)S(1)} %get-tuple-element.18.refs_1_, bf16[512,256]{1,0:T(8,128)(2,1)S(1)} %copy-done.9, bf16[128,128]{1,0:T(8,128)(2,1)S(1)} %collective-permute-done.3.refs_3_.refs_1_.refs_4_), custom_call_target="tpu_custom_call" | custom-call | flops 16777216 | bytes 32768 | tf_op jit(solution)/shard_map/inner_step/pallas_call | solution.py:49
  33.5 1.4 %collective-permute-start.5 = (bf16[128,128]{1,0:T(8,128)(2,1)S(1)}, bf16[128,128]{1,0:T(8,128)(2,1)S(1)}, u32[]{:S(2)}, u32[]{:S(2)}) collective-permute-start(bf16[128,128]{1,0:T(8,128)(2,1)S(1)} %merge.7), channel_id=1, source_target_pairs={{0,16},{4,20},{8,24},{12,28},{16,0},{20,4},{24,8},{28,12},{1,17},{... | collective-permute-start | bytes 98312 | tf_op jit(solution)/shard_map/ppermute | solution.py:437
  34.9 2.6 %collective-permute-done.5.refs_6_ = bf16[128,128]{1,0:T(8,128)(2,1)S(1)} collective-permute-done((bf16[128,128]{1,0:T(8,128)(2,1)S(1)}, bf16[128,128]{1,0:T(8,128)(2,1)S(1)}, u32[]{:S(2)}, u32[]{:S(2)}) %collective-permute-start.5) | collective-permute-done | bytes 32800 | tf_op jit(solution)/shard_map/ppermute | solution.py:437
  39.3 5.4 %weight_send.1 = bf16[4,768,512]{2,1,0:T(8,128)(2,1)} custom-call(s32[1]{0:T(128)} %bitcast.10.refs_0_, bf16[512,4096]{1,0:T(8,128)(2,1)} %refs_1_.25, bf16[768,512]{1,0:T(8,128)(2,1)} %copy-done.3), custom_call_target="tpu_custom_call" | custom-call | flops 25165824 | bytes 81920 | tf_op jit(solution)/shard_map/weight_send/pallas_call | solution.py:49
  45.5 2.2 %copy-done = bf16[4096,512]{1,0:T(8,128)(2,1)S(1)} copy-done((bf16[4096,512]{1,0:T(8,128)(2,1)S(1)}, bf16[4096,512]{1,0:T(8,128)(2,1)}, u32[]{:S(2)}) %copy-start) | copy-done | bytes 4194328
  49.1 1.4 %partial.11.refs_4_ = bf16[1024,256]{1,0:T(8,128)(2,1)S(1)} custom-call(s32[5]{0:T(128)S(1)} %dynamic-slice_bitcast_fusion.refs_0_, bf16[4096,512]{1,0:T(8,128)(2,1)S(1)} %copy-done, bf16[4096,256]{1,0:T(8,128)(2,1)S(1)} %copy-done.2, bf16[768,512]{1,0:T(8,128)(2,1)S(1)} %copy-done.4), custom_call_target="tpu_custom_call" | custom-call | flops 6291456 | bytes 40960 | tf_op jit(solution)/shard_map/partial/pallas_call | solution.py:49
  51.3 5.3 %weight_keep.1 = (bf16[2,768,512]{2,1,0:T(8,128)(2,1)S(1)}, bf16[2,768,512]{2,1,0:T(8,128)(2,1)S(1)}) custom-call(s32[4]{0:T(128)S(1)} %pad_add_fusion.1.refs_0_, bf16[512,4096]{1,0:T(8,128)(2,1)S(1)} %copy-done.5, bf16[768,512]{1,0:T(8,128)(2,1)S(1)} %copy-done.4, bf16[4,768,512]{2,1,0:T(8,128)(2,1)} %collective-permute-done.16.refs_3_, ...), custom_call_target="tpu_custom_call" | custom-call | flops 25165824 | bytes 131072 | tf_op jit(solution)/shard_map/weight_keep/pallas_call | solution.py:49
  56.6 1.4 %collective-permute-start.17 = (bf16[2,768,512]{2,1,0:T(8,128)(2,1)S(1)}, bf16[2,768,512]{2,1,0:T(8,128)(2,1)S(1)}, u32[]{:S(2)}, u32[]{:S(2)}) collective-permute-start(bf16[2,768,512]{2,1,0:T(8,128)(2,1)S(1)} %get-tuple-element.22), channel_id=1, source_target_pairs={{0,16},{4,20},{8,24},{12,28},{16,0},{20,4},{24,8},{28,12},{1,17},{... | collective-permute-start | bytes 4718600 | tf_op jit(solution)/shard_map/ppermute | solution.py:437
  58.0 3.5 %collective-permute-start.11 = (bf16[1024,256]{1,0:T(8,128)(2,1)S(1)}, bf16[1024,256]{1,0:T(8,128)(2,1)S(1)}, u32[]{:S(2)}, u32[]{:S(2)}) collective-permute-start(bf16[1024,256]{1,0:T(8,128)(2,1)S(1)} %partial.16.refs_5_), channel_id=1, source_target_pairs={{0,1},{3,2},{4,5},{7,6},{8,9},{11,10},{12,13},{15,14},{16,17},{19,... | collective-permute-start | bytes 1572872 | tf_op jit(solution)/shard_map/ppermute | solution.py:576
  62.8 10.9 %collective-permute-done.11.refs_4_ = bf16[1024,256]{1,0:T(8,128)(2,1)S(1)} collective-permute-done((bf16[1024,256]{1,0:T(8,128)(2,1)S(1)}, bf16[1024,256]{1,0:T(8,128)(2,1)S(1)}, u32[]{:S(2)}, u32[]{:S(2)}) %collective-permute-start.11) | collective-permute-done | bytes 524320 | tf_op jit(solution)/shard_map/ppermute | solution.py:576
  73.7 1.4 %partial.17 = bf16[1024,256]{1,0:T(8,128)(2,1)S(1)} custom-call(s32[5]{0:T(128)S(1)} %dynamic-slice_bitcast_fusion.refs_0_, bf16[4096,512]{1,0:T(8,128)(2,1)S(1)} %copy-done.1, bf16[4096,256]{1,0:T(8,128)(2,1)S(1)} %copy-done.2, bf16[768,512]{1,0:T(8,128)(2,1)S(1)} %copy-done.4, bf16[1024,256]{1,0:T(8,128)(2,1)S(1)} %collective-permute-done.11.refs_4_), custom_call_target="tpu_custom_call" | custom-call | flops 6291456 | bytes 40960 | tf_op jit(solution)/shard_map/partial/pallas_call | solution.py:49
  75.8 5.0 %collective-permute-start.12 = (bf16[1024,256]{1,0:T(8,128)(2,1)S(1)}, bf16[1024,256]{1,0:T(8,128)(2,1)S(1)}, u32[]{:S(2)}, u32[]{:S(2)}) collective-permute-start(bf16[1024,256]{1,0:T(8,128)(2,1)S(1)} %partial.17), channel_id=1, source_target_pairs={{0,1},{1,2},{4,5},{5,6},{8,9},{9,10},{12,13},{13,14},{16,17},{17,1... | collective-permute-start | bytes 1572872 | tf_op jit(solution)/shard_map/ppermute | solution.py:536
  80.8 4.1 %collective-permute-done.6.refs_4_ = bf16[1024,256]{1,0:T(8,128)(2,1)S(1)} collective-permute-done((bf16[1024,256]{1,0:T(8,128)(2,1)S(1)}, bf16[1024,256]{1,0:T(8,128)(2,1)S(1)}, u32[]{:S(2)}, u32[]{:S(2)}) %collective-permute-start.6) | collective-permute-done | bytes 524320 | tf_op jit(solution)/shard_map/ppermute | solution.py:576
  84.9 1.4 %partial.12 = bf16[1024,256]{1,0:T(8,128)(2,1)S(1)} custom-call(s32[5]{0:T(128)S(1)} %dynamic-slice_bitcast_fusion.refs_0_, bf16[4096,512]{1,0:T(8,128)(2,1)S(1)} %copy-done.1, bf16[4096,256]{1,0:T(8,128)(2,1)S(1)} %copy-done.2, bf16[768,512]{1,0:T(8,128)(2,1)S(1)} %copy-done.4, bf16[1024,256]{1,0:T(8,128)(2,1)S(1)} %collective-permute-done.6.refs_4_), custom_call_target="tpu_custom_call" | custom-call | flops 6291456 | bytes 40960 | tf_op jit(solution)/shard_map/partial/pallas_call | solution.py:49
  87.0 5.2 %collective-permute-start.7 = (bf16[1024,256]{1,0:T(8,128)(2,1)S(1)}, bf16[1024,256]{1,0:T(8,128)(2,1)S(1)}, u32[]{:S(2)}, u32[]{:S(2)}) collective-permute-start(bf16[1024,256]{1,0:T(8,128)(2,1)S(1)} %partial.12), channel_id=1, source_target_pairs={{0,1},{1,2},{4,5},{5,6},{8,9},{9,10},{12,13},{13,14},{16,17},{17,1... | collective-permute-start | bytes 1572872 | tf_op jit(solution)/shard_map/ppermute | solution.py:536
  94.4 1.4 %partial.19 = bf16[1024,256]{1,0:T(8,128)(2,1)S(1)} custom-call(s32[5]{0:T(128)S(1)} %dynamic-slice_bitcast_fusion.refs_0_, bf16[4096,512]{1,0:T(8,128)(2,1)S(1)} %copy-done.1, bf16[4096,256]{1,0:T(8,128)(2,1)S(1)} %copy-done.2, bf16[768,512]{1,0:T(8,128)(2,1)S(1)} %copy-done.4, bf16[1024,256]{1,0:T(8,128)(2,1)S(1)} %collective-permute-done.14.refs_4_), custom_call_target="tpu_custom_call" | custom-call | flops 6291456 | bytes 40960 | tf_op jit(solution)/shard_map/partial/pallas_call | solution.py:49
  97.1 1.4 %partial.18 = bf16[1024,256]{1,0:T(8,128)(2,1)S(1)} custom-call(s32[5]{0:T(128)S(1)} %dynamic-slice_bitcast_fusion.refs_0_, bf16[4096,512]{1,0:T(8,128)(2,1)S(1)} %copy-done.1, bf16[4096,256]{1,0:T(8,128)(2,1)S(1)} %copy-done.2, bf16[768,512]{1,0:T(8,128)(2,1)S(1)} %copy-done.4, bf16[1024,256]{1,0:T(8,128)(2,1)S(1)} %collective-permute-done.12.refs_4_), custom_call_target="tpu_custom_call" | custom-call | flops 6291456 | bytes 40960 | tf_op jit(solution)/shard_map/partial/pallas_call | solution.py:49
  98.4 4.6 %collective-permute-start.13 = (bf16[1024,256]{1,0:T(8,128)(2,1)S(1)}, bf16[1024,256]{1,0:T(8,128)(2,1)S(1)}, u32[]{:S(2)}, u32[]{:S(2)}) collective-permute-start(bf16[1024,256]{1,0:T(8,128)(2,1)S(1)} %partial.18), channel_id=1, source_target_pairs={{0,1},{1,2},{2,3},{4,5},{5,6},{6,7},{8,9},{9,10},{10,11},{12,13},{... | collective-permute-start | bytes 1572872 | tf_op jit(solution)/shard_map/ppermute | solution.py:536
  103.0 1.4 %partial.14 = bf16[1024,256]{1,0:T(8,128)(2,1)S(1)} custom-call(s32[5]{0:T(128)S(1)} %dynamic-slice_bitcast_fusion.refs_0_, bf16[4096,512]{1,0:T(8,128)(2,1)S(1)} %copy-done.1, bf16[4096,256]{1,0:T(8,128)(2,1)S(1)} %copy-done.2, bf16[768,512]{1,0:T(8,128)(2,1)S(1)} %copy-done.4, bf16[1024,256]{1,0:T(8,128)(2,1)S(1)} %collective-permute-done.9.refs_4_), custom_call_target="tpu_custom_call" | custom-call | flops 6291456 | bytes 40960 | tf_op jit(solution)/shard_map/partial/pallas_call | solution.py:49
  105.7 1.7 %collective-permute-done.7.refs_4_ = bf16[1024,256]{1,0:T(8,128)(2,1)S(1)} collective-permute-done((bf16[1024,256]{1,0:T(8,128)(2,1)S(1)}, bf16[1024,256]{1,0:T(8,128)(2,1)S(1)}, u32[]{:S(2)}, u32[]{:S(2)}) %collective-permute-start.7) | collective-permute-done | bytes 524320 | tf_op jit(solution)/shard_map/ppermute | solution.py:536
  107.4 1.4 %partial.13 = bf16[1024,256]{1,0:T(8,128)(2,1)S(1)} custom-call(s32[5]{0:T(128)S(1)} %dynamic-slice_bitcast_fusion.refs_0_, bf16[4096,512]{1,0:T(8,128)(2,1)S(1)} %copy-done.1, bf16[4096,256]{1,0:T(8,128)(2,1)S(1)} %copy-done.2, bf16[768,512]{1,0:T(8,128)(2,1)S(1)} %copy-done.4, bf16[1024,256]{1,0:T(8,128)(2,1)S(1)} %collective-permute-done.7.refs_4_), custom_call_target="tpu_custom_call" | custom-call | flops 6291456 | bytes 40960 | tf_op jit(solution)/shard_map/partial/pallas_call | solution.py:49
  108.8 4.7 %collective-permute-start.8 = (bf16[1024,256]{1,0:T(8,128)(2,1)S(1)}, bf16[1024,256]{1,0:T(8,128)(2,1)S(1)}, u32[]{:S(2)}, u32[]{:S(2)}) collective-permute-start(bf16[1024,256]{1,0:T(8,128)(2,1)S(1)} %partial.13), channel_id=1, source_target_pairs={{0,1},{1,2},{2,3},{4,5},{5,6},{6,7},{8,9},{9,10},{10,11},{12,13},{... | collective-permute-start | bytes 1572872 | tf_op jit(solution)/shard_map/ppermute | solution.py:536
  116.2 1.5 %weight_last.1 = (f32[512,512]{1,0:T(8,128)}, f32[1024,128]{1,0:T(8,128)}) custom-call(bf16[1,768,512]{2,1,0:T(8,128)(2,1)S(1)} %get-tuple-element.23.refs_0_, bf16[1,768,512]{2,1,0:T(8,128)(2,1)S(1)} %collective-permute-done.18.refs_1_), custom_call_target="tpu_custom_call" | custom-call | flops 4096 | bytes 32768 | tf_op jit(solution)/shard_map/weight_last/pallas_call | solution.py:49
  118.6 3.5 %collective-permute-done.10.refs_2_ = bf16[1024,256]{1,0:T(8,128)(2,1)S(1)} collective-permute-done((bf16[1024,256]{1,0:T(8,128)(2,1)S(1)}, bf16[1024,256]{1,0:T(8,128)(2,1)S(1)}, u32[]{:S(2)}, u32[]{:S(2)}) %collective-permute-start.10) | collective-permute-done | bytes 524320 | tf_op jit(solution)/shard_map/ppermute | solution.py:536
  122.2 7.0 %collective-permute-done.8.refs_1_ = bf16[1024,256]{1,0:T(8,128)(2,1)S(1)} collective-permute-done((bf16[1024,256]{1,0:T(8,128)(2,1)S(1)}, bf16[1024,256]{1,0:T(8,128)(2,1)S(1)}, u32[]{:S(2)}, u32[]{:S(2)}) %collective-permute-start.8) | collective-permute-done | bytes 524320 | tf_op jit(solution)/shard_map/ppermute | solution.py:536
  130.4 1.5 %final.1 = bf16[512,1024]{1,0:T(8,128)(2,1)} custom-call(bf16[1024,256]{1,0:T(8,128)(2,1)S(1)} %partial.10.refs_0_, bf16[1024,256]{1,0:T(8,128)(2,1)S(1)} %collective-permute-done.8.refs_1_, bf16[1024,256]{1,0:T(8,128)(2,1)S(1)} %collective-permute-done.10.refs_2_, bf16[1024,256]{1,0:T(8,128)(2,1)S(1)} %partial.15.refs_3_, ...), custom_call_target="tpu_custom_call" | custom-call | flops 8192 | bytes 65536 | tf_op jit(solution)/shard_map/final/pallas_call | solution.py:49
  (66 shorter events, 24.6 us)
Async XLA Ops:
  7.4 1.5 %collective-permute-start = (bf16[128,128]{1,0:T(8,128)(2,1)}, bf16[128,128]{1,0:T(8,128)(2,1)S(1)}, u32[]{:S(2)}, u32[]{:S(2)}) collective-permute-start(bf16[128,128]{1,0:T(8,128)(2,1)} %get-tuple-element.16.refs_0_), channel_id=1, source_target_pairs={{0,4},{4,0},{8,12},{12,8},{16,20},{20,16},{24,28},{28,24},{1,5},{5... | collective-permute-start | bytes 98312 | tf_op jit(solution)/shard_map/ppermute | solution.py:437
  9.7 2.9 %copy-start.12 = (bf16[128,128]{1,0:T(8,128)(2,1)}, bf16[128,128]{1,0:T(8,128)(2,1)S(1)}, u32[]{:S(2)}) copy-start(bf16[128,128]{1,0:T(8,128)(2,1)S(1)} %collective-permute-done.refs_2_.refs_1_.refs_6_) | copy-start | bytes 98308
  9.7 9.4 %collective-permute-start.1 = (bf16[128,128]{1,0:T(8,128)(2,1)S(1)}, bf16[128,128]{1,0:T(8,128)(2,1)S(1)}, u32[]{:S(2)}, u32[]{:S(2)}) collective-permute-start(bf16[128,128]{1,0:T(8,128)(2,1)S(1)} %merge.4.refs_0_), channel_id=1, source_target_pairs={{0,8},{4,12},{8,0},{12,4},{16,24},{20,28},{24,16},{28,20},{1,9},{5... | collective-permute-start | bytes 98312 | tf_op jit(solution)/shard_map/ppermute | solution.py:437
  12.6 9.2 %copy-start.9 = (bf16[512,256]{1,0:T(8,128)(2,1)S(1)}, bf16[512,256]{1,0:T(8,128)(2,1)}, u32[]{:S(2)}) copy-start(bf16[512,256]{1,0:T(8,128)(2,1)} %get-tuple-element.17.refs_1_.refs_3_.refs_2_) | copy-start | bytes 786436
  12.6 11.7 %copy-start.11 = (bf16[512,512]{1,0:T(8,128)(2,1)S(1)}, bf16[512,512]{1,0:T(8,128)(2,1)}, u32[]{:S(2)}) copy-start(bf16[512,512]{1,0:T(8,128)(2,1)} %refs_5_.1) | copy-start | bytes 1572868
  20.1 4.2 %copy-start.8 = (bf16[512,512]{1,0:T(8,128)(2,1)S(1)}, bf16[512,512]{1,0:T(8,128)(2,1)}, u32[]{:S(2)}) copy-start(bf16[512,512]{1,0:T(8,128)(2,1)} %q_project.1.refs_0_.refs_2_.refs_1_) | copy-start | bytes 1572868
  20.1 4.2 %copy-start.13 = (bf16[128,128]{1,0:T(8,128)(2,1)S(1)}, bf16[128,128]{1,0:T(8,128)(2,1)}, u32[]{:S(2)}) copy-start(bf16[128,128]{1,0:T(8,128)(2,1)} %copy-done.12) | copy-start | bytes 98308
  20.1 4.2 %copy-start.15 = (f32[512]{0:T(512)S(1)}, f32[512]{0:T(512)}, u32[]{:S(2)}) copy-start(f32[512]{0:T(512)} %param.9) | copy-start | bytes 6148
  20.1 4.1 %collective-permute-start.2 = (bf16[128,128]{1,0:T(8,128)(2,1)S(1)}, bf16[128,128]{1,0:T(8,128)(2,1)S(1)}, u32[]{:S(2)}, u32[]{:S(2)}) collective-permute-start(bf16[128,128]{1,0:T(8,128)(2,1)S(1)} %merge.5), channel_id=1, source_target_pairs={{0,16},{4,20},{8,24},{12,28},{16,0},{20,4},{24,8},{28,12},{1,17},{... | collective-permute-start | bytes 98312 | tf_op jit(solution)/shard_map/ppermute | solution.py:437
  21.8 1.0 copy-start.7
  28.2 1.3 collective-permute-start.3
  29.5 4.0 %collective-permute-start.4 = (bf16[128,128]{1,0:T(8,128)(2,1)S(1)}, bf16[128,128]{1,0:T(8,128)(2,1)S(1)}, u32[]{:S(2)}, u32[]{:S(2)}) collective-permute-start(bf16[128,128]{1,0:T(8,128)(2,1)S(1)} %merge.6.refs_0_), channel_id=1, source_target_pairs={{0,8},{4,12},{8,0},{12,4},{16,24},{20,28},{24,16},{28,20},{1,9},{5... | collective-permute-start | bytes 98312 | tf_op jit(solution)/shard_map/ppermute | solution.py:437
  33.5 4.0 %collective-permute-start.5 = (bf16[128,128]{1,0:T(8,128)(2,1)S(1)}, bf16[128,128]{1,0:T(8,128)(2,1)S(1)}, u32[]{:S(2)}, u32[]{:S(2)}) collective-permute-start(bf16[128,128]{1,0:T(8,128)(2,1)S(1)} %merge.7), channel_id=1, source_target_pairs={{0,16},{4,20},{8,24},{12,28},{16,0},{20,4},{24,8},{28,12},{1,17},{... | collective-permute-start | bytes 98312 | tf_op jit(solution)/shard_map/ppermute | solution.py:437
  39.3 6.2 %copy-start.2 = (bf16[4096,256]{1,0:T(8,128)(2,1)S(1)}, bf16[4096,256]{1,0:T(8,128)(2,1)}, u32[]{:S(2)}) copy-start(bf16[4096,256]{1,0:T(8,128)(2,1)} %get-tuple-element.15.refs_2_) | copy-start | bytes 6291460
  39.3 6.2 %copy-start.4 = (bf16[768,512]{1,0:T(8,128)(2,1)S(1)}, bf16[768,512]{1,0:T(8,128)(2,1)}, u32[]{:S(2)}) copy-start(bf16[768,512]{1,0:T(8,128)(2,1)} %copy-done.3) | copy-start | bytes 2359300
  44.7 6.0 %collective-permute-start.16 = (bf16[4,768,512]{2,1,0:T(8,128)(2,1)}, bf16[4,768,512]{2,1,0:T(8,128)(2,1)}, u32[]{:S(2)}, u32[]{:S(2)}) collective-permute-start(bf16[4,768,512]{2,1,0:T(8,128)(2,1)} %weight_send.1), channel_id=1, source_target_pairs={{0,4},{4,0},{8,12},{12,8},{16,20},{20,16},{24,28},{28,24},{1,5},{5... | collective-permute-start | bytes 9437192 | tf_op jit(solution)/shard_map/ppermute | solution.py:437
  45.5 2.2 %copy-start = (bf16[4096,512]{1,0:T(8,128)(2,1)S(1)}, bf16[4096,512]{1,0:T(8,128)(2,1)}, u32[]{:S(2)}) copy-start(bf16[4096,512]{1,0:T(8,128)(2,1)} %refs_1_.23) | copy-start | bytes 12582916
  49.1 2.2 %copy-start.5 = (bf16[512,4096]{1,0:T(8,128)(2,1)S(1)}, bf16[512,4096]{1,0:T(8,128)(2,1)}, u32[]{:S(2)}) copy-start(bf16[512,4096]{1,0:T(8,128)(2,1)} %refs_1_.25) | copy-start | bytes 12582916
  51.3 22.4 %copy-start.1 = (bf16[4096,512]{1,0:T(8,128)(2,1)S(1)}, bf16[4096,512]{1,0:T(8,128)(2,1)}, u32[]{:S(2)}) copy-start(bf16[4096,512]{1,0:T(8,128)(2,1)} %refs_1_.23) | copy-start | bytes 12582916
  56.6 36.9 %collective-permute-start.17 = (bf16[2,768,512]{2,1,0:T(8,128)(2,1)S(1)}, bf16[2,768,512]{2,1,0:T(8,128)(2,1)S(1)}, u32[]{:S(2)}, u32[]{:S(2)}) collective-permute-start(bf16[2,768,512]{2,1,0:T(8,128)(2,1)S(1)} %get-tuple-element.22), channel_id=1, source_target_pairs={{0,16},{4,20},{8,24},{12,28},{16,0},{20,4},{24,8},{28,12},{1,17},{... | collective-permute-start | bytes 4718600 | tf_op jit(solution)/shard_map/ppermute | solution.py:437
  58.0 15.7 %collective-permute-start.11 = (bf16[1024,256]{1,0:T(8,128)(2,1)S(1)}, bf16[1024,256]{1,0:T(8,128)(2,1)S(1)}, u32[]{:S(2)}, u32[]{:S(2)}) collective-permute-start(bf16[1024,256]{1,0:T(8,128)(2,1)S(1)} %partial.16.refs_5_), channel_id=1, source_target_pairs={{0,1},{3,2},{4,5},{7,6},{8,9},{11,10},{12,13},{15,14},{16,17},{19,... | collective-permute-start | bytes 1572872 | tf_op jit(solution)/shard_map/ppermute | solution.py:576
  61.5 23.5 %collective-permute-start.6 = (bf16[1024,256]{1,0:T(8,128)(2,1)S(1)}, bf16[1024,256]{1,0:T(8,128)(2,1)S(1)}, u32[]{:S(2)}, u32[]{:S(2)}) collective-permute-start(bf16[1024,256]{1,0:T(8,128)(2,1)S(1)} %partial.11.refs_4_), channel_id=1, source_target_pairs={{0,1},{3,2},{4,5},{7,6},{8,9},{11,10},{12,13},{15,14},{16,17},{19,... | collective-permute-start | bytes 1572872 | tf_op jit(solution)/shard_map/ppermute | solution.py:576
  75.1 19.3 %collective-permute-start.14 = (bf16[1024,256]{1,0:T(8,128)(2,1)S(1)}, bf16[1024,256]{1,0:T(8,128)(2,1)S(1)}, u32[]{:S(2)}, u32[]{:S(2)}) collective-permute-start(bf16[1024,256]{1,0:T(8,128)(2,1)S(1)} %partial.17), channel_id=1, source_target_pairs={{3,2},{2,1},{7,6},{6,5},{11,10},{10,9},{15,14},{14,13},{19,18},{18... | collective-permute-start | bytes 1572872 | tf_op jit(solution)/shard_map/ppermute | solution.py:536
  75.8 21.3 %collective-permute-start.12 = (bf16[1024,256]{1,0:T(8,128)(2,1)S(1)}, bf16[1024,256]{1,0:T(8,128)(2,1)S(1)}, u32[]{:S(2)}, u32[]{:S(2)}) collective-permute-start(bf16[1024,256]{1,0:T(8,128)(2,1)S(1)} %partial.17), channel_id=1, source_target_pairs={{0,1},{1,2},{4,5},{5,6},{8,9},{9,10},{12,13},{13,14},{16,17},{17,1... | collective-permute-start | bytes 1572872 | tf_op jit(solution)/shard_map/ppermute | solution.py:536
  86.3 16.7 %collective-permute-start.9 = (bf16[1024,256]{1,0:T(8,128)(2,1)S(1)}, bf16[1024,256]{1,0:T(8,128)(2,1)S(1)}, u32[]{:S(2)}, u32[]{:S(2)}) collective-permute-start(bf16[1024,256]{1,0:T(8,128)(2,1)S(1)} %partial.12), channel_id=1, source_target_pairs={{3,2},{2,1},{7,6},{6,5},{11,10},{10,9},{15,14},{14,13},{19,18},{18... | collective-permute-start | bytes 1572872 | tf_op jit(solution)/shard_map/ppermute | solution.py:536
  87.0 20.4 %collective-permute-start.7 = (bf16[1024,256]{1,0:T(8,128)(2,1)S(1)}, bf16[1024,256]{1,0:T(8,128)(2,1)S(1)}, u32[]{:S(2)}, u32[]{:S(2)}) collective-permute-start(bf16[1024,256]{1,0:T(8,128)(2,1)S(1)} %partial.12), channel_id=1, source_target_pairs={{0,1},{1,2},{4,5},{5,6},{8,9},{9,10},{12,13},{13,14},{16,17},{17,1... | collective-permute-start | bytes 1572872 | tf_op jit(solution)/shard_map/ppermute | solution.py:536
  93.8 22.4 %collective-permute-start.18 = (bf16[1,768,512]{2,1,0:T(8,128)(2,1)S(1)}, bf16[1,768,512]{2,1,0:T(8,128)(2,1)S(1)}, u32[]{:S(2)}, u32[]{:S(2)}) collective-permute-start(bf16[1,768,512]{2,1,0:T(8,128)(2,1)S(1)} %get-tuple-element.24), channel_id=1, source_target_pairs={{0,8},{4,12},{8,0},{12,4},{16,24},{20,28},{24,16},{28,20},{1,9},{5... | collective-permute-start | bytes 2359304 | tf_op jit(solution)/shard_map/ppermute | solution.py:437
  95.8 22.0 %collective-permute-start.15 = (bf16[1024,256]{1,0:T(8,128)(2,1)S(1)}, bf16[1024,256]{1,0:T(8,128)(2,1)S(1)}, u32[]{:S(2)}, u32[]{:S(2)}) collective-permute-start(bf16[1024,256]{1,0:T(8,128)(2,1)S(1)} %partial.19), channel_id=1, source_target_pairs={{3,2},{2,1},{1,0},{7,6},{6,5},{5,4},{11,10},{10,9},{9,8},{15,14},{... | collective-permute-start | bytes 1572872 | tf_op jit(solution)/shard_map/ppermute | solution.py:536
  98.4 20.2 %collective-permute-start.13 = (bf16[1024,256]{1,0:T(8,128)(2,1)S(1)}, bf16[1024,256]{1,0:T(8,128)(2,1)S(1)}, u32[]{:S(2)}, u32[]{:S(2)}) collective-permute-start(bf16[1024,256]{1,0:T(8,128)(2,1)S(1)} %partial.18), channel_id=1, source_target_pairs={{0,1},{1,2},{2,3},{4,5},{5,6},{6,7},{8,9},{9,10},{10,11},{12,13},{... | collective-permute-start | bytes 1572872 | tf_op jit(solution)/shard_map/ppermute | solution.py:536
  104.4 17.7 %collective-permute-start.10 = (bf16[1024,256]{1,0:T(8,128)(2,1)S(1)}, bf16[1024,256]{1,0:T(8,128)(2,1)S(1)}, u32[]{:S(2)}, u32[]{:S(2)}) collective-permute-start(bf16[1024,256]{1,0:T(8,128)(2,1)S(1)} %partial.14), channel_id=1, source_target_pairs={{3,2},{2,1},{1,0},{7,6},{6,5},{5,4},{11,10},{10,9},{9,8},{15,14},{... | collective-permute-start | bytes 1572872 | tf_op jit(solution)/shard_map/ppermute | solution.py:536
  108.8 20.4 %collective-permute-start.8 = (bf16[1024,256]{1,0:T(8,128)(2,1)S(1)}, bf16[1024,256]{1,0:T(8,128)(2,1)S(1)}, u32[]{:S(2)}, u32[]{:S(2)}) collective-permute-start(bf16[1024,256]{1,0:T(8,128)(2,1)S(1)} %partial.13), channel_id=1, source_target_pairs={{0,1},{1,2},{2,3},{4,5},{5,6},{6,7},{8,9},{9,10},{10,11},{12,13},{... | collective-permute-start | bytes 1572872 | tf_op jit(solution)/shard_map/ppermute | solution.py:536
  129.2 1.2 copy-start.10
  (3 other events, 2.7 us)
